TPU v7x, 32 devices: a whole 2x2x4 slice. The times are simulated.
32 devices in a mesh: section: 4 (over y, x), dp: 8 (over z, core).
Axes of the slice: x: 2, y: 2, z: 4, core: 2. Of those that a mesh axis runs over, the one named last changes fastest.
Arguments:
- latent_in: bfloat16 [4096, 512], P('dp'), may hold values from 0 to 0.25
- actions: bfloat16 [4, 4096, 64], P('section', 'dp'), may hold values from -1 to 1
- task_ids: int32 [4096], P('dp'), may hold values from 0 to 79
- valid: int32 [4096], P('dp'), may hold values from 0 to 1, as said below
- action_mask: int32 [80, 64], replicated, may hold values from 0 to 1, as said below
- bins: int32 [4, 4096], P('section', 'dp'), may hold values from 0 to 99
- fraction: float32 [4, 4096], P('section', 'dp'), may hold values from 0 to 1
- latent_cot: bfloat16 [4, 4096, 512], P('section', 'dp'), may hold values from -24 to 24
- w_in: bfloat16 [4, 6, 672, 1024], P('section'), may hold values from -0.25 to 0.25
- b_in: bfloat16 [4, 6, 1024], P('section'), may hold values from -1.5 to 1.5
- g_in: bfloat16 [4, 6, 1024], P('section'), may hold values from 0.5 to 1.5
- beta_in: bfloat16 [4, 6, 1024], P('section'), may hold values from -1.5 to 1.5
- w_mid: bfloat16 [4, 6, 1024, 1024], P('section'), may hold values from -0.1875 to 0.1875
- b_mid: bfloat16 [4, 6, 1024], P('section'), may hold values from -1.5 to 1.5
- g_mid: bfloat16 [4, 6, 1024], P('section'), may hold values from 0.5 to 1.5
- beta_mid: bfloat16 [4, 6, 1024], P('section'), may hold values from -1.5 to 1.5
- w_dyn_out: bfloat16 [4, 1024, 512], P('section'), may hold values from -0.75 to 0.75
- b_dyn_out: bfloat16 [4, 512], P('section'), may hold values from -2.5 to 2.5
- g_dyn_out: bfloat16 [4, 512], P('section'), may hold values from 0.5 to 1.5
- beta_dyn_out: bfloat16 [4, 512], P('section'), may hold values from -2.5 to 2.5
- w_q_out: bfloat16 [4, 5, 1024, 101], P('section'), may hold values from -0.375 to 0.375
- b_q_out: bfloat16 [4, 5, 101], P('section'), may hold values from -2.5 to 2.5
- table: bfloat16 [80, 96], replicated, may hold values from -5 to 5
Outputs:
- latents_out: bfloat16 [4, 4096, 512], P('section', 'dp')
- grad_latents: float32 [4, 4096, 512], P('section', 'dp')
- grad_w_in: float32 [4, 6, 672, 1024], P('section', None, None, 'dp')
- grad_b_in: float32 [4, 6, 1024], P('section', None, 'dp')
- grad_g_in: float32 [4, 6, 1024], P('section', None, 'dp')
- grad_beta_in: float32 [4, 6, 1024], P('section', None, 'dp')
- grad_w_mid: float32 [4, 6, 1024, 1024], P('section', None, None, 'dp')
- grad_b_mid: float32 [4, 6, 1024], P('section', None, 'dp')
- grad_g_mid: float32 [4, 6, 1024], P('section', None, 'dp')
- grad_beta_mid: float32 [4, 6, 1024], P('section', None, 'dp')
- grad_w_dyn_out: float32 [4, 1024, 512], P('section', 'dp')
- grad_b_dyn_out: float32 [4, 512], P('section')
- grad_g_dyn_out: float32 [4, 512], P('section')
- grad_beta_dyn_out: float32 [4, 512], P('section')
- grad_w_q_out: float32 [4, 5, 1024, 101], P('section', None, 'dp')
- grad_b_q_out: float32 [4, 5, 101], P('section')
- grad_table: float32 [80, 96], replicated
- rms_stats: float32 [4, 2], P('section')
Inputs may be any that keep to these rules, and one draw needn't show every extreme that they name: `valid`: every aligned block of 512 rows holds a 1. `action_mask`: row t is 1 on its first k_t entries and 0 after them, k_t from 16 to 61, both reached.
All inputs are finite; a program needn't handle non-finite values.
Results may differ from a plain program's by a relative error of at most 0.012.
Values may be sent and summed in bfloat16 or wider, within the bound.
A program may use at most 576 MiB of HBM per device.

v0:
```python
import jax
import jax.numpy as jnp
from jax import lax
from jax.sharding import PartitionSpec as P

GROUP = 8
MICRO = 4


EPS = 1e-05
HIGH_PRECISION = lax.Precision.HIGHEST
FLOAT_THIRTY_TWO = jnp.float32
B16 = jnp.bfloat16


def passed_along(block, axis, distance):
    devices = range(lax.axis_size(axis))
    route = [(i - distance, i) for i in devices if i - distance in devices]
    return lax.ppermute(block, axis, route)


def mish(values):
    return values * jnp.tanh(jax.nn.softplus(values))


def normed(values, gain_vec, shift_vec):
    center = values - jnp.mean(values, -1, keepdims=True)
    spread = jnp.mean(center * center, -1, keepdims=True)
    return mish(center * lax.rsqrt(spread + EPS) * gain_vec[:, None, :] + shift_vec[:, None, :])


def simplex_norm(values, gain_vec, shift_vec):
    center = values - jnp.mean(values, -1, keepdims=True)
    spread = jnp.mean(center * center, -1, keepdims=True)
    scaled = center * lax.rsqrt(spread + EPS) * gain_vec + shift_vec
    row_total = values.shape[0]
    return jax.nn.softmax(scaled.reshape(row_total, -1, GROUP), -1).reshape(row_total, -1)


def put_block(buffer, slot_index, update, active):
    old_value = lax.dynamic_index_in_dim(buffer, slot_index, 0, keepdims=False)
    return lax.dynamic_update_index_in_dim(
        buffer, jnp.where(active, update, old_value), slot_index, 0
    )


def take_block(buffer, slot_index):
    return lax.dynamic_index_in_dim(buffer, slot_index, 0, keepdims=False)


def on_device(
    latent_in,
    actions,
    task_ids,
    valid,
    action_mask,
    bins,
    fraction,
    latent_cot,
    w_in,
    b_in,
    g_in,
    beta_in,
    w_mid,
    b_mid,
    g_mid,
    beta_mid,
    w_dyn_out,
    b_dyn_out,
    g_dyn_out,
    beta_dyn_out,
    w_q_out,
    b_q_out,
    table,
):
    section_count = lax.axis_size("section")
    section_here = lax.axis_index("section")
    row_count = latent_in.shape[0]
    block_rows = row_count // MICRO
    lat_width = latent_in.shape[1]
    in_width = w_in.shape[2]
    hid_width = w_mid.shape[-1]
    head_count = w_in.shape[1]
    bin_count = w_q_out.shape[-1]
    emb_width = table.shape[1]
    weight_in = w_in[0]
    bias_in = b_in[0].astype(FLOAT_THIRTY_TWO)
    gain_in = g_in[0].astype(FLOAT_THIRTY_TWO)
    shift_in = beta_in[0].astype(FLOAT_THIRTY_TWO)
    weight_mid = w_mid[0]
    bias_mid = b_mid[0].astype(FLOAT_THIRTY_TWO)
    gain_mid = g_mid[0].astype(FLOAT_THIRTY_TWO)
    shift_mid = beta_mid[0].astype(FLOAT_THIRTY_TWO)
    weight_dyn = w_dyn_out[0]
    bias_dyn = b_dyn_out[0].astype(FLOAT_THIRTY_TWO)
    gain_dyn = g_dyn_out[0].astype(FLOAT_THIRTY_TWO)
    shift_dyn = beta_dyn_out[0].astype(FLOAT_THIRTY_TWO)
    critic_weight_matrix = w_q_out[0]
    bias_q = b_q_out[0].astype(FLOAT_THIRTY_TWO)
    onehot = (task_ids[:, None] == jnp.arange(table.shape[0], dtype=jnp.int32)[None, :]).astype(B16)
    embedded = jnp.dot(onehot, table, preferred_element_type=FLOAT_THIRTY_TWO)
    act_mask = jnp.dot(onehot, action_mask.astype(B16), preferred_element_type=FLOAT_THIRTY_TWO)
    side_all = jnp.concatenate(
        [(actions[0].astype(FLOAT_THIRTY_TWO) * act_mask).astype(B16), embedded.astype(B16)], 1
    )
    valid_all = valid.astype(FLOAT_THIRTY_TWO)
    bins_all = bins[0]
    frac_all = fraction[0]
    cot_all = latent_cot[0].astype(FLOAT_THIRTY_TWO)
    bin_lanes = jnp.arange(bin_count, dtype=jnp.int32)[None, :]

    def rows_of(source, slot_index):
        return lax.dynamic_slice_in_dim(source, slot_index * block_rows, block_rows, 0)

    kept_buf = (
        jnp.zeros((MICRO, block_rows, in_width), B16),
        jnp.zeros((MICRO, head_count, block_rows, hid_width), FLOAT_THIRTY_TWO),
        jnp.zeros((MICRO, head_count, block_rows, hid_width), B16),
        jnp.zeros((MICRO, head_count, block_rows, hid_width), FLOAT_THIRTY_TWO),
        jnp.zeros((MICRO, head_count, block_rows, hid_width), B16),
        jnp.zeros((MICRO, block_rows, lat_width), FLOAT_THIRTY_TWO),
        jnp.zeros((MICRO, head_count - 1, block_rows, bin_count), B16),
    )
    latent_buf = jnp.zeros((MICRO, block_rows, lat_width), B16)
    stat_sum = jnp.zeros((3,), FLOAT_THIRTY_TWO)
    outgoing = jnp.zeros((block_rows, lat_width), B16)
    for moment in range(MICRO + section_count - 1):
        batch_index = moment - section_here
        active = (batch_index >= 0) & (batch_index < MICRO)
        slot_index = jnp.clip(batch_index, 0, MICRO - 1)
        if moment > 0:
            arrived = passed_along(outgoing, "section", 1)
        else:
            arrived = jnp.zeros_like(outgoing)
        latent = jnp.where(section_here == 0, rows_of(latent_in, slot_index), arrived)
        side = rows_of(side_all, slot_index)
        forward_inputs = jnp.concatenate([latent, side], 1)
        forward_first_pre = (
            jnp.einsum(
                "ri,hij->hrj", forward_inputs, weight_in, preferred_element_type=FLOAT_THIRTY_TWO
            )
            + bias_in[:, None, :]
        )
        forward_first_act = normed(forward_first_pre, gain_in, shift_in).astype(B16)
        forward_second_pre = (
            jnp.einsum(
                "hri,hij->hrj",
                forward_first_act,
                weight_mid,
                preferred_element_type=FLOAT_THIRTY_TWO,
            )
            + bias_mid[:, None, :]
        )
        forward_second_activation = normed(forward_second_pre, gain_mid, shift_mid).astype(B16)
        forward_dyn_pre = (
            jnp.dot(
                forward_second_activation[0], weight_dyn, preferred_element_type=FLOAT_THIRTY_TWO
            )
            + bias_dyn
        )
        new_latent = simplex_norm(forward_dyn_pre, gain_dyn, shift_dyn)
        critic_logits = (
            jnp.einsum(
                "tcy,tyo->tco",
                forward_second_activation[1:],
                critic_weight_matrix,
                preferred_element_type=FLOAT_THIRTY_TWO,
            )
            + bias_q[:, None, :]
        )
        forward_valid_rows = rows_of(valid_all, slot_index)
        bin_rows = rows_of(bins_all, slot_index)
        frac_rows = rows_of(frac_all, slot_index)
        target = (1.0 - frac_rows)[:, None] * (bin_lanes == bin_rows[:, None]).astype(
            FLOAT_THIRTY_TWO
        )
        target = target + frac_rows[:, None] * (bin_lanes == bin_rows[:, None] + 1).astype(
            FLOAT_THIRTY_TWO
        )
        forward_critic_gradient = (
            forward_valid_rows[None, :, None] * (jax.nn.softmax(critic_logits, -1) - target[None])
        ).astype(B16)
        sent_latent = new_latent.astype(B16)
        sent_float = sent_latent.astype(FLOAT_THIRTY_TWO)
        stat = jnp.stack(
            [
                jnp.sum(forward_valid_rows),
                jnp.sum(forward_valid_rows * jnp.sum(sent_float * sent_float, 1)),
                jnp.zeros((), FLOAT_THIRTY_TWO),
            ]
        )
        sent_latent, kept_now, stat = (
            sent_latent,
            (
                forward_inputs,
                forward_first_pre,
                forward_first_act,
                forward_second_pre,
                forward_second_activation,
                forward_dyn_pre,
                forward_critic_gradient,
            ),
            stat,
        )
        kept_buf = tuple(
            (
                put_block(buffer, slot_index, update, active)
                for buffer, update in zip(kept_buf, kept_now)
            )
        )
        latent_buf = put_block(latent_buf, slot_index, sent_latent, active)
        stat_sum = stat_sum + jnp.where(active, stat, 0.0)
        outgoing = sent_latent
    vec_sum = jnp.zeros((6, head_count, hid_width), FLOAT_THIRTY_TWO)
    dyn_vec_sum = jnp.zeros((2, lat_width), FLOAT_THIRTY_TWO)
    dyn_bias_sum = jnp.zeros((lat_width,), FLOAT_THIRTY_TWO)
    q_bias_sum = jnp.zeros((head_count - 1, bin_count), FLOAT_THIRTY_TWO)
    table_sum = jnp.zeros(table.shape, FLOAT_THIRTY_TWO)
    grad_buf = jnp.zeros((MICRO, block_rows, lat_width), FLOAT_THIRTY_TWO)
    stat_lane = (jnp.arange(3, dtype=jnp.int32) == 2).astype(FLOAT_THIRTY_TWO)
    weight_sums = (
        jnp.zeros((hid_width, head_count, in_width), FLOAT_THIRTY_TWO),
        jnp.zeros((hid_width, head_count, hid_width), FLOAT_THIRTY_TWO),
        jnp.zeros((hid_width, lat_width), FLOAT_THIRTY_TWO),
        jnp.zeros((hid_width, head_count - 1, bin_count), FLOAT_THIRTY_TWO),
    )
    back_out = jnp.zeros((block_rows, lat_width), B16)
    for moment in range(MICRO + section_count - 1):
        batch_index = moment - (section_count - 1 - section_here)
        active = (batch_index >= 0) & (batch_index < MICRO)
        slot_index = jnp.clip(batch_index, 0, MICRO - 1)
        if moment > 0:
            arrived = passed_along(back_out, "section", -1)
        else:
            arrived = jnp.zeros_like(back_out)
        grad_sent = rows_of(cot_all, slot_index) + arrived.astype(FLOAT_THIRTY_TWO)
        kept_now = tuple((take_block(buffer, slot_index) for buffer in kept_buf))
        inputs, first_pre, first_act, second_pre, second_activation, dyn_pre, critic_gradient = (
            kept_now
        )
        dyn_back = jax.vjp(simplex_norm, dyn_pre, gain_dyn, shift_dyn)[1]
        dyn_pre_grad, gain_dyn_grad, shift_dyn_grad = dyn_back(grad_sent)
        dyn_grad = dyn_pre_grad.astype(B16)
        act_dyn = jnp.einsum(
            "rc,jc->rj", dyn_grad, weight_dyn, preferred_element_type=FLOAT_THIRTY_TWO
        )
        action_for_critic = jnp.einsum(
            "nvk,nlk->nvl",
            critic_gradient,
            critic_weight_matrix,
            preferred_element_type=FLOAT_THIRTY_TWO,
        )
        second_act_grad = jnp.concatenate([act_dyn[None], action_for_critic], 0)
        second_back = jax.vjp(normed, second_pre, gain_mid, shift_mid)[1]
        second_pre_grad, gain_mid_grad, shift_mid_grad = second_back(second_act_grad)
        second_low = second_pre_grad.astype(B16)
        first_act_grad = jnp.einsum(
            "hrj,hij->hri", second_low, weight_mid, preferred_element_type=FLOAT_THIRTY_TWO
        )
        first_back = jax.vjp(normed, first_pre, gain_in, shift_in)[1]
        first_pre_grad, gain_in_grad, shift_in_grad = first_back(first_act_grad)
        first_low = first_pre_grad.astype(B16)
        inputs_grad = jnp.einsum(
            "hrj,hij->ri", first_low, weight_in, preferred_element_type=FLOAT_THIRTY_TWO
        )
        vectors = jnp.stack(
            [
                jnp.sum(first_low.astype(FLOAT_THIRTY_TWO), 1),
                gain_in_grad,
                shift_in_grad,
                jnp.sum(second_low.astype(FLOAT_THIRTY_TWO), 1),
                gain_mid_grad,
                shift_mid_grad,
            ]
        )
        dyn_vectors = jnp.stack([gain_dyn_grad, shift_dyn_grad])
        inputs_grad, first_low, second_low, dyn_grad, vectors, dyn_vectors = (
            inputs_grad,
            first_low,
            second_low,
            dyn_grad,
            vectors,
            dyn_vectors,
        )
        on_off = jnp.where(active, 1.0, 0.0).astype(FLOAT_THIRTY_TWO)
        latent_grad = inputs_grad[:, :lat_width]
        grad_buf = put_block(grad_buf, slot_index, latent_grad, active)
        back_out = latent_grad.astype(B16)
        valid_rows = rows_of(valid_all, slot_index)
        grad_square = jnp.sum(valid_rows * jnp.sum(latent_grad * latent_grad, 1))
        stat_sum = stat_sum + on_off * grad_square * stat_lane
        vec_sum = vec_sum + on_off * vectors
        dyn_vec_sum = dyn_vec_sum + on_off * dyn_vectors
        dyn_bias_sum = dyn_bias_sum + on_off * jnp.sum(dyn_grad.astype(FLOAT_THIRTY_TWO), 0)
        q_bias_sum = q_bias_sum + on_off * jnp.sum(kept_now[6].astype(FLOAT_THIRTY_TWO), 1)
        emb_grad = inputs_grad[:, in_width - emb_width :]
        hot_rows = rows_of(onehot, slot_index).astype(FLOAT_THIRTY_TWO)
        table_sum = table_sum + on_off * jnp.dot(hot_rows.T, emb_grad, precision=HIGH_PRECISION)
        inputs, first_pre, first_act, second_pre, second_activation, dyn_pre, critic_gradient = (
            kept_now
        )
        weight_sums = (
            weight_sums[0]
            + on_off
            * jnp.einsum("ri,hrj->jhi", inputs, first_low, preferred_element_type=FLOAT_THIRTY_TWO),
            weight_sums[1]
            + on_off
            * jnp.einsum(
                "hri,hrj->jhi", first_act, second_low, preferred_element_type=FLOAT_THIRTY_TWO
            ),
            weight_sums[2]
            + on_off
            * jnp.einsum(
                "rj,rc->jc", second_activation[0], dyn_grad, preferred_element_type=FLOAT_THIRTY_TWO
            ),
            weight_sums[3]
            + on_off
            * jnp.einsum(
                "hrj,hrb->jhb",
                second_activation[1:],
                critic_gradient,
                preferred_element_type=FLOAT_THIRTY_TWO,
            ),
        )
    vectors_t = jnp.transpose(vec_sum, (2, 0, 1)).reshape(hid_width, 6 * head_count)
    local_rows = hid_width // lax.axis_size("dp")
    pieces = [source.reshape(local_rows * lax.axis_size("dp"), -1) for source in weight_sums]
    pieces.append(vectors_t)
    summed = lax.psum_scatter(jnp.concatenate(pieces, 1), "dp", scatter_dimension=0, tiled=True)
    stat_total, dyn_bias_total, dyn_vec_total, q_bias_total = lax.psum(
        (stat_sum, dyn_bias_sum, dyn_vec_sum, q_bias_sum), "dp"
    )
    table_total = lax.psum(table_sum, ("section", "dp"))
    offset_mid = head_count * in_width
    offset_dyn = offset_mid + head_count * hid_width
    offset_q = offset_dyn + lat_width
    offset_vec = offset_q + (head_count - 1) * bin_count
    part_in = (
        summed[:, :offset_mid].reshape(local_rows, head_count, in_width).transpose(1, 2, 0)[None]
    )
    part_mid = (
        summed[:, offset_mid:offset_dyn]
        .reshape(local_rows, head_count, hid_width)
        .transpose(1, 2, 0)[None]
    )
    part_dyn = summed[:, offset_dyn:offset_q][None]
    part_q = (
        summed[:, offset_q:offset_vec]
        .reshape(local_rows, head_count - 1, bin_count)
        .transpose(1, 0, 2)[None]
    )
    vec_part = summed[:, offset_vec:].reshape(local_rows, 6, head_count)
    vec_grads = [jnp.transpose(vec_part[:, kind_index, :])[None] for kind_index in range(6)]
    count_valid = stat_total[0]
    rms_stats = jnp.stack(
        [jnp.sqrt(stat_total[1] / count_valid), jnp.sqrt(stat_total[2] / (count_valid * lat_width))]
    )[None]
    return (
        latent_buf.reshape(1, row_count, lat_width),
        grad_buf.reshape(1, row_count, lat_width),
        part_in,
        vec_grads[0],
        vec_grads[1],
        vec_grads[2],
        part_mid,
        vec_grads[3],
        vec_grads[4],
        vec_grads[5],
        part_dyn,
        dyn_bias_total[None],
        dyn_vec_total[0][None],
        dyn_vec_total[1][None],
        part_q,
        q_bias_total[None],
        table_total,
        rms_stats,
    )


def solution(mesh):
    placed = (
        P("dp", None),
        P("section", "dp", None),
        P("dp"),
        P("dp"),
        P(),
        P("section", "dp"),
        P("section", "dp"),
        P("section", "dp", None),
        P("section", None, None, None),
        P("section", None, None),
        P("section", None, None),
        P("section", None, None),
        P("section", None, None, None),
        P("section", None, None),
        P("section", None, None),
        P("section", None, None),
        P("section", None, None),
        P("section", None),
        P("section", None),
        P("section", None),
        P("section", None, None, None),
        P("section", None, None),
        P(),
    )
    return jax.shard_map(
        on_device,
        mesh=mesh,
        in_specs=placed,
        out_specs=(
            P("section", "dp", None),
            P("section", "dp", None),
            P("section", None, None, "dp"),
            P("section", None, "dp"),
            P("section", None, "dp"),
            P("section", None, "dp"),
            P("section", None, None, "dp"),
            P("section", None, "dp"),
            P("section", None, "dp"),
            P("section", None, "dp"),
            P("section", "dp", None),
            P("section", None),
            P("section", None),
            P("section", None),
            P("section", None, "dp", None),
            P("section", None, None),
            P(),
            P("section", None),
        ),
        check_vma=False,
    )
```

profile of v0, /device:TPU:14, one launch (start us, length us, event | category | flops | bytes accessed | tf_op | source)
XLA Modules:
  0.0 1526.1 jit_solution(3262668370562928347)
XLA Ops:
  13.1 5.0 bitcast_reduce_fusion.6
  43.2 6.1 broadcast.2028.clone.1
  55.4 6.2 broadcast.2028.clone
  91.5 7.8 add_reduce_fusion.5
  365.8 8.5 dynamic-slice_reduce_fusion.1
  377.0 6.7 fusion.718
  383.8 11.3 multiply_reduce_fusion.12
  399.2 9.3 dynamic-slice_reduce_fusion
  411.0 11.3 fusion.719
  422.4 11.8 multiply_reduce_fusion.13
  440.4 7.3 collective-permute-start.6
  458.8 6.1 bitcast_dynamic-update-slice_fusion.21
  464.9 11.7 fusion.200
  478.3 9.0 fusion.505
  493.0 6.1 fusion.720
  506.2 10.1 fusion.198
  516.2 12.3 fusion.721
  537.2 9.0 fusion.503
  559.5 6.3 fusion.722
  572.5 10.0 fusion.196
  582.5 11.9 fusion.723
  603.5 9.0 fusion.501
  625.8 6.6 fusion.724
  639.0 10.1 fusion.194
  649.2 11.9 fusion.725
  670.0 9.2 fusion.499
  679.2 5.3 collective-permute-start.9
  692.4 6.3 fusion.726
  705.4 10.1 fusion.192
  715.5 11.9 fusion.727
  736.5 9.2 fusion.497
  745.6 5.2 collective-permute-start.10
  758.9 6.6 fusion.728
  772.2 10.1 fusion.190
  782.2 10.9 fusion.729
  801.1 9.1 fusion.495
  810.2 5.4 collective-permute-start.11
  820.9 6.3 fusion.730
  832.8 11.1 fusion.731
  849.8 7.0 multiply_add_fusion
  856.8 56.6 %add_add_fusion = f32[6,1024,1024]{1,2,0:T(8,128)} fusion(f32[6,1024,1024]{1,2,0:T(8,128)} %fusion.190, f32[6,1024,1024]{1,2,0:T(8,128)} %fusion.192, f32[6,1024,1024]{1,2,0:T(8,128)} %fusion.194, f32[6,1024,1024]{1,2,0:T(8,128)} %fusion.196, f32[6,1024,1024]{1,2,0:T(8,128)} %fusion.198, f32[6,1024,1024]{1,2,0:T(8,128)} %fusion.200, f32[]{:T(128)S(6)} %select_n.892, ...), kind=kOutput, calls=%fused_computation.21 | convolution fusion | flops 1692401664 | bytes 179306528 | tf_op jit(solution)/shard_map/hri,hrj->jhi/dot_general | solution.py:308
  913.4 38.5 %add_add_fusion.1 = f32[6,1024,672]{1,2,0:T(8,128)} fusion(f32[6,1024,672]{1,2,0:T(8,128)} %fusion.495, f32[6,1024,672]{1,2,0:T(8,128)} %fusion.497, f32[6,1024,672]{1,2,0:T(8,128)} %fusion.499, f32[6,1024,672]{1,2,0:T(8,128)} %fusion.501, f32[6,1024,672]{1,2,0:T(8,128)} %fusion.503, f32[6,1024,672]{1,2,0:T(8,128)} %fusion.505, ...), kind=kOutput, calls=%fused_computation.22 | convolution fusion | flops 1110638592 | bytes 117350432 | tf_op jit(solution)/shard_map/ri,hrj->jhi/dot_general | solution.py:305
  951.9 104.5 %concatenate.139 = f32[1024,11229]{0,1:T(8,128)} concatenate(f32[1024,4032]{0,1:T(8,128)} %bitcast.2001, f32[1024,6144]{0,1:T(8,128)} %bitcast.2000, f32[1024,512]{0,1:T(8,128)} %multiply_add_fusion, f32[1024,505]{0,1:T(8,128)} %reshape.2266, f32[1024,36]{0,1:T(8,128)S(1)} %reshape.2267), dimensions={1} | concatenate | bytes 91987968 | tf_op jit(solution)/shard_map/concatenate | solution.py:329
  1078.0 5.7 fusion.247
  1089.0 9.3 select_add_fusion.7
  1098.5 13.7 all-reduce
  1117.9 48.9 %psum.38 = f32[80,96]{1,0:T(8,128)} all-reduce(f32[80,96]{1,0:T(8,128)S(1)} %fusion.300), channel_id=1, replica_groups=mesh['section'=4,'dp'=8] {'section','dp'}, use_global_device_ids=true, to_apply=%region_249.251 | all-reduce | flops 7680 | bytes 61440 | tf_op jit(solution)/shard_map/psum | solution.py:333
  1168.0 336.3 %reduce-scatter.2.cloned.1.call-done = f32[128,11229]{0,1:T(8,128)} async-done(((f32[1024,11229]{0,1:T(8,128)}), f32[128,11229]{0,1:T(8,128)}) %reduce-scatter.2.cloned.1.call-update) | async-done | bytes 5749264 | tf_op jit(solution)/shard_map/reduce_scatter | solution.py:329
  (1213 shorter events, 540.1 us)
Async XLA Ops:
  7.2 65.6 %copy-start = (bf16[1,5,1024,101]{2,3,1,0:T(8,128)(2,1)S(1)}, bf16[1,5,1024,101]{2,3,1,0:T(8,128)(2,1)}, u32[]{:S(2)}) copy-start(bf16[1,5,1024,101]{2,3,1,0:T(8,128)(2,1)} %param.44) | copy-start | bytes 3102724
  7.2 1497.0 %reduce-scatter.2.cloned.1.call-start = ((), (), s32[]{:S(2)}) async-start(), calls=%async_computation.1 | async-start | bytes 51757056 | tf_op jit(solution)/shard_map/reduce_scatter | solution.py:329
  38.3 46.8 %collective-permute-start = (bf16[128,512]{0,1:T(8,128)(2,1)}, bf16[128,512]{0,1:T(8,128)(2,1)}, u32[]{:S(2)}, u32[]{:S(2)}) collective-permute-start(bf16[128,512]{0,1:T(8,128)(2,1)} %get-tuple-element.490), channel_id=1, source_target_pairs={{0,8},{8,16},{16,24},{1,9},{9,17},{17,25},{2,10},{10,18},{18,26},{... | collective-permute-start | bytes 393224 | tf_op jit(solution)/shard_map/ppermute | solution.py:19
  109.1 27.5 %collective-permute-start.1 = (bf16[128,512]{0,1:T(8,128)(2,1)S(1)}, bf16[128,512]{0,1:T(8,128)(2,1)S(1)}, u32[]{:S(2)}, u32[]{:S(2)}) collective-permute-start(bf16[128,512]{0,1:T(8,128)(2,1)S(1)} %get-tuple-element.488), channel_id=1, source_target_pairs={{0,8},{8,16},{16,24},{1,9},{9,17},{17,25},{2,10},{10,18},{18,26},{... | collective-permute-start | bytes 393224 | tf_op jit(solution)/shard_map/ppermute | solution.py:19
  112.4 26.5 %slice-start.18 = ((s8[12582912]{0:T(1024)(128)(4,1)}), s8[4194304]{0:T(1024)(128)(4,1)S(1)}, s32[]{:S(2)}) async-start(s8[12582912]{0:T(1024)(128)(4,1)} %bitcast.2097), calls=%async_computation.20 | async-start | bytes 8388608
  151.0 27.4 %collective-permute-start.2 = (bf16[128,512]{0,1:T(8,128)(2,1)S(1)}, bf16[128,512]{0,1:T(8,128)(2,1)S(1)}, u32[]{:S(2)}, u32[]{:S(2)}) collective-permute-start(bf16[128,512]{0,1:T(8,128)(2,1)S(1)} %get-tuple-element.486), channel_id=1, source_target_pairs={{0,8},{8,16},{16,24},{1,9},{9,17},{17,25},{2,10},{10,18},{18,26},{... | collective-permute-start | bytes 393224 | tf_op jit(solution)/shard_map/ppermute | solution.py:19
  154.2 26.4 %slice-start.21 = ((s8[12582912]{0:T(1024)(128)(4,1)}), s8[4194304]{0:T(1024)(128)(4,1)S(1)}, s32[]{:S(2)}) async-start(s8[12582912]{0:T(1024)(128)(4,1)} %bitcast.2099), calls=%async_computation.23 | async-start | bytes 8388608
  192.7 27.4 %collective-permute-start.3 = (bf16[128,512]{0,1:T(8,128)(2,1)S(1)}, bf16[128,512]{0,1:T(8,128)(2,1)S(1)}, u32[]{:S(2)}, u32[]{:S(2)}) collective-permute-start(bf16[128,512]{0,1:T(8,128)(2,1)S(1)} %get-tuple-element.484), channel_id=1, source_target_pairs={{0,8},{8,16},{16,24},{1,9},{9,17},{17,25},{2,10},{10,18},{18,26},{... | collective-permute-start | bytes 393224 | tf_op jit(solution)/shard_map/ppermute | solution.py:19
  196.0 26.4 %slice-start.24 = ((s8[12582912]{0:T(1024)(128)(4,1)}), s8[4194304]{0:T(1024)(128)(4,1)S(1)}, s32[]{:S(2)}) async-start(s8[12582912]{0:T(1024)(128)(4,1)} %bitcast.2101), calls=%async_computation.26 | async-start | bytes 8388608
  234.5 27.5 %collective-permute-start.4 = (bf16[128,512]{0,1:T(8,128)(2,1)S(1)}, bf16[128,512]{0,1:T(8,128)(2,1)S(1)}, u32[]{:S(2)}, u32[]{:S(2)}) collective-permute-start(bf16[128,512]{0,1:T(8,128)(2,1)S(1)} %get-tuple-element.482), channel_id=1, source_target_pairs={{0,8},{8,16},{16,24},{1,9},{9,17},{17,25},{2,10},{10,18},{18,26},{... | collective-permute-start | bytes 393224 | tf_op jit(solution)/shard_map/ppermute | solution.py:19
  238.0 26.4 %slice-start.27 = ((s8[12582912]{0:T(1024)(128)(4,1)}), s8[4194304]{0:T(1024)(128)(4,1)S(1)}, s32[]{:S(2)}) async-start(s8[12582912]{0:T(1024)(128)(4,1)} %bitcast.2103), calls=%async_computation.29 | async-start | bytes 8388608
  276.4 27.4 %collective-permute-start.5 = (bf16[128,512]{0,1:T(8,128)(2,1)S(1)}, bf16[128,512]{0,1:T(8,128)(2,1)S(1)}, u32[]{:S(2)}, u32[]{:S(2)}) collective-permute-start(bf16[128,512]{0,1:T(8,128)(2,1)S(1)} %get-tuple-element.480), channel_id=1, source_target_pairs={{0,8},{8,16},{16,24},{1,9},{9,17},{17,25},{2,10},{10,18},{18,26},{... | collective-permute-start | bytes 393224 | tf_op jit(solution)/shard_map/ppermute | solution.py:19
  279.7 26.5 %slice-start.30 = ((s8[12582912]{0:T(1024)(128)(4,1)}), s8[4194304]{0:T(1024)(128)(4,1)S(1)}, s32[]{:S(2)}) async-start(s8[12582912]{0:T(1024)(128)(4,1)} %bitcast.2105), calls=%async_computation.32 | async-start | bytes 8388608
  329.2 23.3 %copy-start.45 = (bf16[4,5,128,101]{2,3,1,0:T(8,128)(2,1)}, bf16[4,5,128,101]{2,3,1,0:T(8,128)(2,1)S(1)}, u32[]{:S(2)}) copy-start(bf16[4,5,128,101]{2,3,1,0:T(8,128)(2,1)S(1)} %constant_dynamic-update-slice_fusion.42) | copy-start | bytes 1551364
  395.1 54.0 %copy-start.164 = (f32[6,128]{1,0:T(8,128)}, f32[6,128]{1,0:T(8,128)S(1)}, u32[]{:S(2)}) copy-start(f32[6,128]{1,0:T(8,128)S(1)} %get-tuple-element.121) | copy-start | bytes 9220
  395.1 55.2 %copy-start.160 = (f32[6,128]{1,0:T(8,128)}, f32[6,128]{1,0:T(8,128)S(1)}, u32[]{:S(2)}) copy-start(f32[6,128]{1,0:T(8,128)S(1)} %get-tuple-element.120) | copy-start | bytes 9220
  399.2 37.9 %slice-start.10 = ((s8[8257536]{0:T(1024)(128)(4,1)}), s8[4063232]{0:T(1024)(128)(4,1)S(1)}, s32[]{:S(2)}) async-start(s8[8257536]{0:T(1024)(128)(4,1)} %bitcast.1992), calls=%async_computation.12 | async-start | bytes 8126464
  411.0 26.1 %slice-start.11 = ((s8[8257536]{0:T(1024)(128)(4,1)}), s8[4194304]{0:T(1024)(128)(4,1)S(1)}, s32[]{:S(2)}) async-start(s8[8257536]{0:T(1024)(128)(4,1)} %bitcast.1992), calls=%async_computation.13 | async-start | bytes 8388608
  440.4 47.1 %collective-permute-start.6 = (bf16[128,512]{0,1:T(8,128)(2,1)S(1)}, bf16[128,512]{0,1:T(8,128)(2,1)S(1)}, u32[]{:S(2)}, u32[]{:S(2)}) collective-permute-start(bf16[128,512]{0,1:T(8,128)(2,1)S(1)} %slice.361), channel_id=1, source_target_pairs={{8,0},{16,8},{24,16},{9,1},{17,9},{25,17},{10,2},{18,10},{26,18},{... | collective-permute-start | bytes 393224 | tf_op jit(solution)/shard_map/ppermute | solution.py:19
  487.5 125.0 %copy-start.205 = (f32[128]{0:T(128)}, f32[128]{0:T(128)S(1)}, u32[]{:S(2)}) copy-start(f32[128]{0:T(128)S(1)} %fusion.695) | copy-start | bytes 1540
  506.1 28.7 %slice-start.12 = ((s8[8257536]{0:T(1024)(128)(4,1)}), s8[4194304]{0:T(1024)(128)(4,1)S(1)}, s32[]{:S(2)}) async-start(s8[8257536]{0:T(1024)(128)(4,1)} %bitcast.1994), calls=%async_computation.14 | async-start | bytes 8388608
  516.2 18.6 %slice-start.13 = ((s8[8257536]{0:T(1024)(128)(4,1)}), s8[4063232]{0:T(1024)(128)(4,1)S(1)}, s32[]{:S(2)}) async-start(s8[8257536]{0:T(1024)(128)(4,1)} %bitcast.1994), calls=%async_computation.15 | async-start | bytes 8126464
  546.3 7.5 collective-permute-start.7
  613.1 7.3 collective-permute-start.8
  679.2 7.8 collective-permute-start.9
  745.6 7.7 collective-permute-start.10
  810.2 7.9 collective-permute-start.11
  1077.7 20.5 %copy-start.217 = (f32[512]{0:T(512)S(1)}, f32[512]{0:T(512)}, u32[]{:S(2)}) copy-start(f32[512]{0:T(512)} %get-tuple-element.174) | copy-start | bytes 6148
  1077.7 20.5 %copy-start.218 = (f32[512]{0:T(512)S(1)}, f32[512]{0:T(512)}, u32[]{:S(2)}) copy-start(f32[512]{0:T(512)} %get-tuple-element.225) | copy-start | bytes 6148
  1077.8 20.5 %copy-start.220 = (f32[512]{0:T(512)S(1)}, f32[512]{0:T(512)}, u32[]{:S(2)}) copy-start(f32[512]{0:T(512)} %get-tuple-element.176) | copy-start | bytes 6148
  1077.8 20.5 %copy-start.221 = (f32[512]{0:T(512)S(1)}, f32[512]{0:T(512)}, u32[]{:S(2)}) copy-start(f32[512]{0:T(512)} %get-tuple-element.226) | copy-start | bytes 6148
  1077.8 20.5 %copy-start.223 = (f32[512]{0:T(512)S(1)}, f32[512]{0:T(512)}, u32[]{:S(2)}) copy-start(f32[512]{0:T(512)} %get-tuple-element.178) | copy-start | bytes 6148
  1077.8 20.5 %copy-start.224 = (f32[512]{0:T(512)S(1)}, f32[512]{0:T(512)}, u32[]{:S(2)}) copy-start(f32[512]{0:T(512)} %get-tuple-element.227) | copy-start | bytes 6148
  1077.8 20.5 %copy-start.226 = (f32[512]{0:T(512)S(1)}, f32[512]{0:T(512)}, u32[]{:S(2)}) copy-start(f32[512]{0:T(512)} %get-tuple-element.180) | copy-start | bytes 6148
  1077.8 20.5 %copy-start.227 = (f32[512]{0:T(512)S(1)}, f32[512]{0:T(512)}, u32[]{:S(2)}) copy-start(f32[512]{0:T(512)} %get-tuple-element.228) | copy-start | bytes 6148
  1077.8 20.5 %copy-start.229 = (f32[512]{0:T(512)S(1)}, f32[512]{0:T(512)}, u32[]{:S(2)}) copy-start(f32[512]{0:T(512)} %get-tuple-element.182) | copy-start | bytes 6148
  1077.8 20.5 %copy-start.230 = (f32[512]{0:T(512)S(1)}, f32[512]{0:T(512)}, u32[]{:S(2)}) copy-start(f32[512]{0:T(512)} %get-tuple-element.229) | copy-start | bytes 6148
  1077.8 20.5 %copy-start.232 = (f32[512]{0:T(512)S(1)}, f32[512]{0:T(512)}, u32[]{:S(2)}) copy-start(f32[512]{0:T(512)} %get-tuple-element.184) | copy-start | bytes 6148
  1077.9 20.5 %copy-start.233 = (f32[512]{0:T(512)S(1)}, f32[512]{0:T(512)}, u32[]{:S(2)}) copy-start(f32[512]{0:T(512)} %get-tuple-element.230) | copy-start | bytes 6148
  1077.9 20.5 %copy-start.235 = (f32[512]{0:T(512)S(1)}, f32[512]{0:T(512)}, u32[]{:S(2)}) copy-start(f32[512]{0:T(512)} %get-tuple-element.186) | copy-start | bytes 6148
  1077.9 20.5 %copy-start.236 = (f32[512]{0:T(512)S(1)}, f32[512]{0:T(512)}, u32[]{:S(2)}) copy-start(f32[512]{0:T(512)} %get-tuple-element.231) | copy-start | bytes 6148
  1077.9 20.6 %copy-start.216 = (f32[512]{0:T(512)S(1)}, f32[512]{0:T(512)}, u32[]{:S(2)}) copy-start(f32[512]{0:T(512)} %get-tuple-element.264) | copy-start | bytes 6148
  1077.9 20.5 %copy-start.219 = (f32[512]{0:T(512)S(1)}, f32[512]{0:T(512)}, u32[]{:S(2)}) copy-start(f32[512]{0:T(512)} %get-tuple-element.266) | copy-start | bytes 6148
  1077.9 20.5 %copy-start.222 = (f32[512]{0:T(512)S(1)}, f32[512]{0:T(512)}, u32[]{:S(2)}) copy-start(f32[512]{0:T(512)} %get-tuple-element.268) | copy-start | bytes 6148
  1077.9 20.5 %copy-start.225 = (f32[512]{0:T(512)S(1)}, f32[512]{0:T(512)}, u32[]{:S(2)}) copy-start(f32[512]{0:T(512)} %get-tuple-element.270) | copy-start | bytes 6148
  1077.9 20.5 %copy-start.228 = (f32[512]{0:T(512)S(1)}, f32[512]{0:T(512)}, u32[]{:S(2)}) copy-start(f32[512]{0:T(512)} %get-tuple-element.272) | copy-start | bytes 6148
  1077.9 20.5 %copy-start.231 = (f32[512]{0:T(512)S(1)}, f32[512]{0:T(512)}, u32[]{:S(2)}) copy-start(f32[512]{0:T(512)} %get-tuple-element.274) | copy-start | bytes 6148
  1078.0 20.5 %copy-start.234 = (f32[512]{0:T(512)S(1)}, f32[512]{0:T(512)}, u32[]{:S(2)}) copy-start(f32[512]{0:T(512)} %get-tuple-element.276) | copy-start | bytes 6148
  (271 other events, 1882.8 us)
Sparse Core Ops, SparseCore 0:
  1056.6 447.5 reduce-scatter.1
where the time goes:
time: 1540 us; the launch traced here: 1530 us
  matrix products  440 us (29%)
  waiting for transfers between devices  348 us (23%)
  other arithmetic  346 us (22%)
  local copies, waits for them, and re-layouts  259 us (17%)
  blocking collectives  62.7 us (4%)
  starting transfers between devices  42.7 us (3%)
  between operations  27.4 us (2%)
    reduce_scatter x1, waiting for transfers between devices, on_device(): lax.psum_scatter(jnp.concatenate(pieces, 1), 'dp', scatter_dimension=0, t...  336 us
    dot_general x7, matrix products, on_device(): jnp.einsum('hri,hrj->jhi', first_act, second_low, preferred_element_type=...  119 us
    dynamic_update_slice x41, other arithmetic, put_block(): lax.dynamic_update_index_in_dim(buffer, jnp.where(active, update, old_val...  112 us
    reduce_sum x21, other arithmetic, normed(): center * lax.rsqrt(spread + EPS) * gain_vec[:, None, :]  106 us
    concatenate x1, local copies, waits for them, and re-layouts, on_device(): jnp.concatenate(pieces, 1)  105 us
    dot_general x7, matrix products, on_device(): jnp.einsum('ri,hrj->jhi', inputs, first_low, preferred_element_type=FLOAT...  92.9 us
    dynamic_slice x42, local copies, waits for them, and re-layouts, put_block(): old_value = lax.dynamic_index_in_dim(buffer, slot_index, 0, keepdims=False)  81.9 us
    dot_general x7, matrix products, on_device(): jnp.einsum('hrj,hij->hri', second_low, weight_mid, preferred_element_type...  81.3 us
  transfers between devices with their start and end apart: 13, of which 6 were waited for; matrix products, arithmetic and copies ran while one was open for 16% of the time, Pallas kernels for 0%

commit v1 on v0

v1 whole, which is shorter than its diff:
```python
import functools

import jax
import jax.numpy as jnp
from jax import lax
from jax.experimental import pallas as pl
from jax.experimental.pallas import tpu as pltpu
from jax.sharding import PartitionSpec as P

GROUP = 8
EPS = 1e-05
F32 = jnp.float32
B16 = jnp.bfloat16
MESH = pl.DeviceIdType.MESH

LANES = 128
CHIPS = 4
PEERS = 2 * CHIPS
CHUNK = 128
QROWS = 256
SUB = 128
VECS = 16

NN = (((1,), (0,)), ((), ()))
NT = (((1,), (1,)), ((), ()))
TN = (((0,), (0,)), ((), ()))


def dot(a, b, dims=NN):
    return lax.dot_general(a, b, dims, preferred_element_type=F32)


def split_dot(a, b, dims=NN):
    high = a.astype(B16)
    low = (a - high.astype(F32)).astype(B16)
    return dot(high, b, dims) + dot(low, b, dims)


def split_dot_right(a, b, dims):
    high = b.astype(B16)
    low = (b - high.astype(F32)).astype(B16)
    return dot(a, high, dims) + dot(a, low, dims)


def norm_mish(x, gain, shift):
    center = x - jnp.mean(x, -1, keepdims=True)
    spread = jnp.mean(center * center, -1, keepdims=True)
    scale = lax.rsqrt(spread + EPS)
    n = center * scale
    u = n * gain + shift
    w = jnp.exp(jnp.minimum(u, 30.0))
    top = w * (w + 2.0)
    over = pltpu.reciprocal(top + 2.0, approx=True)
    act = u * (top * over)
    slope = (top + 4.0 * (u * (top - w)) * over) * over
    return act, n, slope, scale


def tiles(size, step=256):
    return [(lo, min(lo + step, size)) for lo in range(0, size, step)]


def eight_rows(x):
    return x.reshape(x.shape[0] // 8, 8, x.shape[1]).sum(0)


def each_sub(count, body):
    if count <= SUB:
        body(0, count)
        return

    def step(j, carry):
        body(pl.multiple_of(j * SUB, SUB), SUB)
        return carry

    lax.fori_loop(0, count // SUB, step, 0)


def layer_forward(pre, count, bias, gain, shift, act_ref, act_at, n_ref, slope_ref, scale_ref, lane, at):
    def body(j, sub):
        act, n, slope, scale = norm_mish(pre[pl.ds(j, sub), :] + bias, gain, shift)
        act_ref[pl.ds(act_at + j, sub), :] = act.astype(B16)
        here = pl.ds(at + j, sub)
        n_ref[here, :] = n.astype(n_ref.dtype)
        slope_ref[here, :] = slope.astype(slope_ref.dtype)
        scale_ref[here, lane : lane + 1] = scale

    each_sub(count, body)


def layer_backward(pre, count, gain, n_ref, slope_ref, scale_ref, lane, at, out_ref, out_at, sums, first):
    def body(j, sub):
        here = pl.ds(at + j, sub)
        n = n_ref[here, :].astype(F32)
        du = pre[pl.ds(j, sub), :] * slope_ref[here, :].astype(F32)
        by_n = du * n
        dn = du * gain
        mean_dn = jnp.mean(dn, -1, keepdims=True)
        mean_by_n = jnp.mean(by_n * gain, -1, keepdims=True)
        out = (dn - mean_dn - n * mean_by_n) * scale_ref[here, lane : lane + 1]
        out_ref[pl.ds(out_at + j, sub), :] = out.astype(B16)
        sums[first : first + 8, :] += eight_rows(out)
        sums[first + 8 : first + 16, :] += eight_rows(by_n)
        sums[first + 16 : first + 24, :] += eight_rows(du)

    each_sub(count, body)


def step_kernel(dims, *refs):
    rows, lat, act_width, in_width, hid, heads, bins, tasks, emb, steps = dims
    side_width = in_width - lat
    block = in_width + hid + LANES + VECS
    block0 = in_width + hid + lat + VECS
    at_mid = in_width
    at_out = in_width + hid
    (
        lat_in, acts, meta, amask, table, cot_in, w_in, w_mid, w_dyn, w_q,
        b_in, g_in, s_in, b_mid, g_mid, s_mid, b_dyn, g_dyn, s_dyn, b_q,
        lat_out, grad_out, recv_q, recv_0, small_out,
        x, m, hot, wi, wm, wq, wq_raw, wi0, wm0, wd, vec, bq, diag,
        ig, act1, act2, spg, fpg, qg, n1, d1, n2, d2, q_scales, pre,
        act1_0, act2_0, spg_0, fpg_0, n1_0, d1_0, n2_0, d2_0, scales,
        dyn_n, new_lat, lat_low, cot, dyn_grad, arrived, back, pair_grad, pair_send,
        gb, half_q, half_0, sums, q_sums, dyn_sums, stat, small, small_recv, table_recv,
        w_sem, in_sem, out_sem, lat_s, lat_r, px_s, px_r, side_s, side_r, pg_s, pg_r, gr_s, gr_r,
        half_s, half_r, own_s, rb_s, rb_r, sm_s, sm_r, tb_s, tb_r,
    ) = refs
    section = lax.axis_index("section")
    d = lax.axis_index("dp")
    place = lax.rem(d, PEERS)
    base = d - place
    chip = place // 2
    core = lax.rem(place, 2)
    edge = (chip == 0) | (chip == CHIPS - 1)
    last = steps - 1
    mate = base + chip * 2 + (1 - core)
    pair = base + (chip + 1 - 2 * lax.rem(chip, 2)) * 2 + core
    following = jnp.minimum(section + 1, last)
    before = jnp.maximum(section - 1, 0)
    chunks = rows // CHUNK
    head_of = [jnp.int32(3), jnp.where(edge, 1, 4), jnp.where(edge, 2, 5)]

    def remote(src, dst, send, recv, to):
        return pltpu.make_async_remote_copy(
            src_ref=src, dst_ref=dst, send_sem=send, recv_sem=recv, device_id=to, device_id_type=MESH
        )

    def chunk_at(i):
        return pl.multiple_of(i * CHUNK, CHUNK)

    loads = [
        pltpu.make_async_copy(w_in.at[0], wi0, w_sem.at[0]),
        pltpu.make_async_copy(w_mid.at[0], wm0, w_sem.at[1]),
        pltpu.make_async_copy(w_dyn, wd, w_sem.at[2]),
    ]
    for job in range(3):
        h = head_of[job]
        slot = job % 2
        loads += [
            pltpu.make_async_copy(w_in.at[h], wi.at[slot], w_sem.at[3 + 3 * job]),
            pltpu.make_async_copy(w_mid.at[h], wm.at[slot], w_sem.at[4 + 3 * job]),
            pltpu.make_async_copy(w_q.at[h - 1], wq_raw.at[slot], w_sem.at[5 + 3 * job]),
        ]
    load_cot = pltpu.make_async_copy(cot_in, cot, w_sem.at[12])
    load_meta = pltpu.make_async_copy(meta, m.at[0:rows], w_sem.at[13])
    load_meta.start()

    def load_lat(i):
        here = pl.ds(chunk_at(i), CHUNK)
        return pltpu.make_async_copy(lat_in.at[here], x.at[here, 0:lat], in_sem.at[i])

    for copy in loads[:1]:
        copy.start()

    @pl.when(section == 0)
    def _():
        for i in range(chunks):
            load_lat(i).start()

    for copy in loads[1:9]:
        copy.start()
    load_cot.start()

    barrier = pltpu.get_barrier_semaphore()
    for other in range(1, PEERS):
        to = base + lax.rem(place + other, PEERS)
        pl.semaphore_signal(barrier, inc=1, device_id=(section, to), device_id_type=MESH)
    for other in range(1, steps):
        to = lax.rem(section + other, steps)
        pl.semaphore_signal(barrier, inc=1, device_id=(to, d), device_id_type=MESH)

    load_meta.wait()
    one_hot = (m[0:rows, 0:1] == lax.broadcasted_iota(jnp.int32, (rows, tasks), 1).astype(F32)).astype(B16)
    hot[0:rows, :] = one_hot
    mask = dot(one_hot, amask[...].astype(F32).astype(B16))
    side = jnp.concatenate(
        [(acts[...].astype(F32) * mask).astype(B16), dot(one_hot, table[...]).astype(B16)], 1
    )
    x[0:rows, lat:in_width] = side
    for t, source in enumerate((b_in, g_in, s_in, b_mid, g_mid, s_mid)):
        vec[t, 0 : heads + 1, :] = source[...].astype(F32)
    bq[...] = jnp.full(bq.shape, -1e30, F32)
    bq[0:heads, 0:bins] = b_q[...].astype(F32)
    wq[...] = jnp.zeros(wq.shape, B16)
    shift = GROUP.bit_length() - 1
    diag[...] = (
        lax.shift_right_logical(lax.broadcasted_iota(jnp.int32, (lat, lat), 0), shift)
        == lax.shift_right_logical(lax.broadcasted_iota(jnp.int32, (lat, lat), 1), shift)
    ).astype(F32).astype(B16)
    sums[...] = jnp.zeros(sums.shape, F32)
    ig[rows : 2 * rows, :] = jnp.zeros((rows, in_width), F32)
    q_sums[...] = jnp.zeros(q_sums.shape, F32)
    dyn_sums[...] = jnp.zeros(dyn_sums.shape, F32)
    stat[...] = jnp.zeros(stat.shape, F32)
    small[...] = jnp.zeros(small.shape, F32)

    @pl.when(section == last)
    def _():
        arrived[...] = jnp.zeros(arrived.shape, B16)

    pl.semaphore_wait(barrier, PEERS - 1 + steps - 1)

    side_copy = remote(
        x.at[0:rows, lat : lat + 2 * LANES], x.at[rows : 2 * rows, lat : lat + 2 * LANES],
        side_s.at[0], side_r.at[0], (section, pair),
    )
    meta_copy = remote(
        m.at[0:rows], m.at[rows : 2 * rows], side_s.at[1], side_r.at[1], (section, pair)
    )
    side_copy.start()
    meta_copy.start()
    for copy in loads[:3]:
        copy.wait()

    def vec_of(t, h):
        return vec[t, pl.ds(h, 1), :]

    def lat_copy(i):
        here = pl.ds(chunk_at(i), CHUNK)
        return remote(
            lat_low.at[here], x.at[here, 0:lat], lat_s.at[i], lat_r.at[i], (following, d)
        )

    def pair_copy(i):
        here = chunk_at(i)
        return remote(
            x.at[pl.ds(here, CHUNK), 0:lat], x.at[pl.ds(rows + here, CHUNK), 0:lat],
            px_s.at[i], px_r.at[i], (section, pair),
        )

    def lat_store(i):
        here = pl.ds(chunk_at(i), CHUNK)
        return pltpu.make_async_copy(lat_low.at[here], lat_out.at[here], out_sem.at[i])

    def forward_chunk(i, carry):
        at = chunk_at(i)
        here = pl.ds(at, CHUNK)

        @pl.when(section > 0)
        def _():
            lat_copy(i).wait_recv()

        @pl.when(section == 0)
        def _():
            load_lat(i).wait()

        pair_copy(i).start()
        pre[0:CHUNK, :] = dot(x[here, 0:in_width], wi0[...])
        layer_forward(
            pre, CHUNK, vec[0, 0:1, :], vec[1, 0:1, :], vec[2, 0:1, :], act1_0, at, n1_0, d1_0, scales, 0, at
        )
        pre[0:CHUNK, :] = dot(act1_0[here, :], wm0[...])
        layer_forward(
            pre, CHUNK, vec[3, 0:1, :], vec[4, 0:1, :], vec[5, 0:1, :], act2_0, at, n2_0, d2_0, scales, 1, at
        )
        out = dot(act2_0[here, :], wd[...]) + b_dyn[...].astype(F32)
        center = out - jnp.mean(out, -1, keepdims=True)
        scale = lax.rsqrt(jnp.mean(center * center, -1, keepdims=True) + EPS)
        normal = center * scale
        dyn_n[here, :] = normal
        scales[here, 2:3] = scale
        power = jnp.exp(normal * g_dyn[...].astype(F32) + s_dyn[...].astype(F32))
        fresh = power * pltpu.reciprocal(split_dot(power, diag[...]), approx=True)
        new_lat[here, :] = fresh
        low = fresh.astype(B16)
        lat_low[here, :] = low

        @pl.when(section < last)
        def _():
            lat_copy(i).start()

        lat_store(i).start()
        wide = low.astype(F32)
        stat[0:8, :] += eight_rows(m[here, 1:2] * (wide * wide))
        return carry

    lax.fori_loop(0, chunks, forward_chunk, 0)

    def q_chunk(job, at):
        here = pl.ds(at, QROWS)
        h = head_of[job]
        pre[...] = dot(x[here, 0:in_width], wi[job % 2])
        layer_forward(
            pre, QROWS, vec_of(0, h), vec_of(1, h), vec_of(2, h), act1, at, n1, d1, q_scales, 0, 0
        )
        pre[...] = dot(act1[here, :], wm[job % 2])
        layer_forward(
            pre, QROWS, vec_of(3, h), vec_of(4, h), vec_of(5, h), act2, at, n2, d2, q_scales, 1, 0
        )
        logits = dot(act2[here, :], wq[job % 2]) + bq[pl.ds(h - 1, 1), :]
        power = jnp.exp(logits - jnp.max(logits, -1, keepdims=True))
        chance = power / jnp.sum(power, -1, keepdims=True)
        lane = lax.broadcasted_iota(jnp.int32, (QROWS, LANES), 1).astype(F32)
        low_bin = m[here, 2:3]
        part = m[here, 3:4]
        target = jnp.where(lane == low_bin, 1.0 - part, 0.0) + jnp.where(lane == low_bin + 1.0, part, 0.0)
        grad = (m[here, 1:2] * (chance - target)).astype(B16)
        qg[here, :] = grad
        q_sums[8 * job : 8 * job + 8, :] += eight_rows(grad.astype(F32))
        pre[...] = dot(grad, wq[job % 2], NT)
        layer_backward(pre, QROWS, vec_of(4, h), n2, d2, q_scales, 1, 0, spg, at, sums.at[job], 24)
        pre[...] = dot(spg[here, :], wm[job % 2], NT)
        layer_backward(pre, QROWS, vec_of(1, h), n1, d1, q_scales, 0, 0, fpg, at, sums.at[job], 0)
        for lo, hi in tiles(in_width):
            back_in = dot(fpg[here, :], wi[job % 2, lo:hi, :], NT)
            if job == 0:
                ig[here, lo:hi] = back_in
            else:
                ig[here, lo:hi] += back_in

    def q_job(job):
        for copy in loads[3 + 3 * job : 6 + 3 * job]:
            copy.wait()
        wq[job % 2, :, 0:bins] = wq_raw[job % 2]

        def body(i, carry):
            q_chunk(job, pl.multiple_of(i * QROWS, QROWS))
            return carry

        lax.fori_loop(0, (rows if job == 0 else 2 * rows) // QROWS, body, 0)

    def half_copy(job, z):
        if job < 3:
            src, dst = gb.at[1 - core, z, 0:block], half_q.at[job, z]
        else:
            src, dst = gb.at[1 - core, z], half_0.at[z]
        return remote(src, dst, half_s.at[job, z], half_r.at[job, z], (section, mate))

    def owner_copy(job, z):
        if job < 3:
            src, dst = half_q.at[job, z], recv_q.at[job, chip]
        else:
            src, dst = half_0.at[z], recv_0.at[chip]
        return remote(src, dst, rb_s.at[job, z], rb_r.at[job, chip], (section, base + 2 * z + core))

    def arrival(job, z):
        if job < 3:
            src, dst = half_q.at[job, chip], recv_q.at[job, z]
        else:
            src, dst = half_0.at[chip], recv_0.at[z]
        return remote(src, dst, rb_s.at[job, z], rb_r.at[job, z], (section, base + 2 * z + core))

    def keep_copy(job):
        if job < 3:
            src, dst = half_q.at[job, chip], recv_q.at[job, chip]
        else:
            src, dst = half_0.at[chip], recv_0.at[chip]
        return pltpu.make_async_copy(src, dst, own_s.at[job])

    def weight_grads(job):
        if job < 3:
            count = rows if job == 0 else 2 * rows
            a1, a2, sp, fp, out = act1, act2, spg, fpg, qg
        else:
            count = rows
            a1, a2, sp, fp, out = act1_0, act2_0, spg_0, fpg_0, dyn_grad
        size = block if job < 3 else block0

        def body(z, carry):
            cols = pl.ds(pl.multiple_of(z * 2 * LANES, 2 * LANES), 2 * LANES)
            for left, right, first, size_of in ((x, fp, 0, in_width), (a1, sp, at_mid, hid)):
                for lo, hi in tiles(size_of):
                    grad = dot(left[0:count, lo:hi], right[0:count, cols], TN)
                    for p in range(2):
                        gb[p, z, first + lo : first + hi, :] = grad[:, p * LANES : (p + 1) * LANES].astype(B16)
            g_out = dot(a2[0:count, cols], out[0:count, :], TN)
            for p in range(2):
                for t in range(g_out.shape[1] // LANES):
                    gb[p, z, at_out + t * LANES : at_out + (t + 1) * LANES, :] = g_out[
                        p * LANES : (p + 1) * LANES, t * LANES : (t + 1) * LANES
                    ].astype(B16)
            lines = [jnp.sum(sums[job, 8 * t : 8 * t + 8, cols], 0, keepdims=True) for t in range(6)]
            lines.append(jnp.zeros((VECS - 6, 2 * LANES), F32))
            vectors = jnp.concatenate(lines, 0).astype(B16)
            for p in range(2):
                gb[p, z, size - VECS : size, :] = vectors[:, p * LANES : (p + 1) * LANES]
            half_copy(job, z).start()
            return carry

        lax.fori_loop(0, CHIPS, body, 0)

        def finish(z, carry):
            half_copy(job, z).wait_recv()
            parts = 4
            step = size // parts // 16 * 16
            for part in range(parts):
                span = slice(part * step, size if part == parts - 1 else (part + 1) * step)
                if job < 3:
                    half_q[job, z, span, :] = (
                        half_q[job, z, span, :].astype(F32) + gb[core, z, span, :].astype(F32)
                    ).astype(B16)
                else:
                    half_0[z, span, :] = (
                        half_0[z, span, :].astype(F32) + gb[core, z, span, :].astype(F32)
                    ).astype(B16)

            @pl.when(z != chip)
            def _():
                owner_copy(job, z).start()

            return carry

        lax.fori_loop(0, CHIPS, finish, 0)
        keep_copy(job).start()

        def sent(z, carry):
            half_copy(job, z).wait_send()
            return carry

        lax.fori_loop(0, CHIPS, sent, 0)

    q_job(0)
    for copy in loads[9:]:
        copy.start()
    weight_grads(0)

    side_copy.wait_recv()
    meta_copy.wait_recv()
    hot[rows : 2 * rows, :] = (
        m[rows : 2 * rows, 0:1] == lax.broadcasted_iota(jnp.int32, (rows, tasks), 1).astype(F32)
    ).astype(B16)

    def pair_here(i, carry):
        pair_copy(i).wait_recv()
        return carry

    lax.fori_loop(0, chunks, pair_here, 0)
    q_job(1)
    weight_grads(1)
    q_job(2)

    def pg_copy(i):
        here = pl.ds(chunk_at(i), CHUNK)
        return remote(
            pair_send.at[here], pair_grad.at[here], pg_s.at[i], pg_r.at[i], (section, pair)
        )

    def send_pair(i, carry):
        at = chunk_at(i)
        pair_send[pl.ds(at, CHUNK), :] = ig[pl.ds(rows + at, CHUNK), 0:lat].astype(B16)
        pg_copy(i).start()
        return carry

    lax.fori_loop(0, chunks, send_pair, 0)

    load_cot.wait()

    def back_copy(i):
        here = pl.ds(chunk_at(i), CHUNK)
        return remote(back.at[here], arrived.at[here], gr_s.at[i], gr_r.at[i], (before, d))

    def grad_store(i):
        here = pl.ds(chunk_at(i), CHUNK)
        return pltpu.make_async_copy(new_lat.at[here], grad_out.at[here], out_sem.at[chunks + i])

    def backward_chunk(i, carry):
        at = chunk_at(i)
        here = pl.ds(at, CHUNK)

        @pl.when(section < last)
        def _():
            back_copy(i).wait_recv()

        out_grad = cot[here, :].astype(F32) + arrived[here, :].astype(F32)
        fresh = new_lat[here, :]
        normal = dyn_n[here, :]
        norm_grad = fresh * (out_grad - split_dot(out_grad * fresh, diag[...]))
        by_n = norm_grad * normal
        gain = g_dyn[...].astype(F32)
        dm = norm_grad * gain
        mean_dm = jnp.mean(dm, -1, keepdims=True)
        mean_by_n = jnp.mean(by_n * gain, -1, keepdims=True)
        low = ((dm - mean_dm - normal * mean_by_n) * scales[here, 2:3]).astype(B16)
        dyn_grad[here, :] = low
        dyn_sums[0:8, :] += eight_rows(low.astype(F32))
        dyn_sums[8:16, :] += eight_rows(by_n)
        dyn_sums[16:24, :] += eight_rows(norm_grad)
        pre[0:CHUNK, :] = dot(low, wd[...], NT)
        layer_backward(pre, CHUNK, vec[4, 0:1, :], n2_0, d2_0, scales, 1, at, spg_0, at, sums.at[3], 24)
        pre[0:CHUNK, :] = dot(spg_0[here, :], wm0[...], NT)
        layer_backward(pre, CHUNK, vec[1, 0:1, :], n1_0, d1_0, scales, 0, at, fpg_0, at, sums.at[3], 0)
        back_in = dot(fpg_0[here, :], wi0[...], NT)
        pg_copy(i).wait_recv()
        total = back_in[:, 0:lat] + ig[here, 0:lat] + pair_grad[here, :].astype(F32)
        back[here, :] = total.astype(B16)

        @pl.when(section > 0)
        def _():
            back_copy(i).start()

        new_lat[here, :] = total
        grad_store(i).start()
        stat[8:16, :] += eight_rows(m[here, 1:2] * (total * total))
        ig[here, lat:in_width] += back_in[:, lat:in_width]
        return carry

    def late(turn, carry):
        @pl.when((turn == 0) == (section == last))
        def _():
            lax.fori_loop(0, chunks, backward_chunk, 0)

        @pl.when((turn == 0) == (section < last))
        def _():
            weight_grads(2)

        return carry

    lax.fori_loop(0, 2, late, 0)
    weight_grads(3)

    small[0:tasks, 0:emb] = split_dot_right(hot[...], ig[:, lat:in_width], TN)[:, side_width - emb :]
    for t in range(3):
        line = jnp.sum(dyn_sums[8 * t : 8 * t + 8, :], 0, keepdims=True)
        for part in range(lat // LANES):
            row = tasks + t * (lat // LANES) + part
            small[row : row + 1, :] = line[:, part * LANES : (part + 1) * LANES]
    q_lines = [jnp.sum(q_sums[8 * job : 8 * job + 8, :], 0, keepdims=True) for job in range(3)]
    for h in range(heads):
        line = sum(jnp.where(head_of[job] == h + 1, q_lines[job], 0.0) for job in range(3))
        row = tasks + 3 * (lat // LANES) + h
        small[row : row + 1, :] = line
    row = tasks + 3 * (lat // LANES) + heads
    lane = lax.broadcasted_iota(jnp.int32, (1, LANES), 1)
    count = jnp.sum(m[0:rows, 1:2], 0, keepdims=True)
    lat_square = jnp.sum(jnp.sum(stat[0:8, :], 0, keepdims=True), 1, keepdims=True)
    grad_square = jnp.sum(jnp.sum(stat[8:16, :], 0, keepdims=True), 1, keepdims=True)
    small[row : row + 1, :] = jnp.where(
        lane == 0, count, jnp.where(lane == 1, lat_square, jnp.where(lane == 2, grad_square, 0.0))
    )
    small_recv[place] = small[...]

    def small_copy(other):
        to = base + lax.rem(place + other, PEERS)
        return remote(small, small_recv.at[place], sm_s.at[other], sm_r.at[place], (section, to))

    def small_arrival(other):
        source = lax.rem(place + other, PEERS)
        return remote(small, small_recv.at[source], sm_s.at[other], sm_r.at[source], (section, base + source))

    for other in range(1, PEERS):
        small_copy(other).start()
    for other in range(1, PEERS):
        small_arrival(other).wait_recv()
    total = small_recv[0]
    for source in range(1, PEERS):
        total = total + small_recv[source]
    for other in range(1, PEERS):
        small_copy(other).wait_send()
    small[...] = total
    table_recv[section] = small[0:tasks, :]

    def table_copy(other):
        to = lax.rem(section + other, steps)
        return remote(
            small.at[0:tasks], table_recv.at[section], tb_s.at[other], tb_r.at[section], (to, d)
        )

    def table_arrival(other):
        source = lax.rem(section + other, steps)
        return remote(small.at[0:tasks], table_recv.at[source], tb_s.at[other], tb_r.at[source], (source, d))

    for other in range(1, steps):
        table_copy(other).start()

    def own_done(job):
        def body(other, carry):
            z = lax.rem(chip + other, CHIPS)
            arrival(job, z).wait_recv()
            owner_copy(job, z).wait_send()
            return carry

        lax.fori_loop(1, CHIPS, body, 0)
        keep_copy(job).wait()

    side_copy.wait_send()
    meta_copy.wait_send()

    def sends(i, carry):
        pair_copy(i).wait_send()
        pg_copy(i).wait_send()
        lat_store(i).wait()
        grad_store(i).wait()

        @pl.when(section < last)
        def _():
            lat_copy(i).wait_send()

        @pl.when(section > 0)
        def _():
            back_copy(i).wait_send()

        return carry

    lax.fori_loop(0, chunks, sends, 0)
    for job in range(4):
        own_done(job)
    for other in range(1, steps):
        table_arrival(other).wait_recv()
    for other in range(1, steps):
        table_copy(other).wait_send()
    whole = table_recv[0]
    for source in range(1, steps):
        whole = whole + table_recv[source]
    small[0:tasks, :] = whole
    done = pltpu.make_async_copy(small, small_out, out_sem.at[2 * chunks])
    done.start()
    done.wait()


def on_device(
    latent_in, actions, task_ids, valid, action_mask, bins, fraction, latent_cot,
    w_in, b_in, g_in, beta_in, w_mid, b_mid, g_mid, beta_mid,
    w_dyn_out, b_dyn_out, g_dyn_out, beta_dyn_out, w_q_out, b_q_out, table,
):
    steps = lax.axis_size("section")
    spread = lax.axis_size("dp")
    groups = spread // PEERS
    rows, lat = latent_in.shape
    act_width = actions.shape[2]
    in_width, hid = w_in.shape[2:]
    heads = w_q_out.shape[1]
    bin_count = w_q_out.shape[-1]
    tasks, emb = table.shape
    block = in_width + hid + LANES + VECS
    block0 = in_width + hid + lat + VECS
    chunks = rows // CHUNK
    small_rows = tasks + 24
    meta = jnp.stack(
        [task_ids.astype(F32), valid.astype(F32), bins[0].astype(F32), fraction[0]], 1
    )
    meta = jnp.pad(meta, ((0, 0), (0, LANES - 4)))
    dims = (rows, lat, act_width, in_width, hid, heads, bin_count, tasks, emb, steps)
    anywhere = pl.BlockSpec(memory_space=pl.ANY)
    vmem = pl.BlockSpec(memory_space=pltpu.VMEM)
    dma = pltpu.SemaphoreType.DMA
    both = 2 * rows
    wide = pltpu.VMEM((rows, hid), B16)
    thin = pltpu.VMEM((rows, LANES), F32)
    low = pltpu.VMEM((rows, lat), B16)
    full = pltpu.VMEM((rows, lat), F32)
    part_low = pltpu.VMEM((QROWS, hid), B16)
    part_thin = pltpu.VMEM((QROWS, LANES), F32)
    q_wide = pltpu.VMEM((both, hid), B16)
    lat_out, grad_out, recv_q, recv_0, small = pl.pallas_call(
        functools.partial(step_kernel, dims),
        out_shape=[
            jax.ShapeDtypeStruct((rows, lat), B16),
            jax.ShapeDtypeStruct((rows, lat), F32),
            jax.ShapeDtypeStruct((3, CHIPS, block, LANES), B16),
            jax.ShapeDtypeStruct((CHIPS, block0, LANES), B16),
            jax.ShapeDtypeStruct((small_rows, LANES), F32),
        ],
        in_specs=[
            anywhere, vmem, anywhere, vmem, vmem, anywhere, anywhere, anywhere, anywhere, anywhere,
            vmem, vmem, vmem, vmem, vmem, vmem, vmem, vmem, vmem, vmem,
        ],
        out_specs=[anywhere] * 5,
        scratch_shapes=[
            pltpu.VMEM((both, 6 * LANES), B16),
            pltpu.VMEM((both, LANES), F32),
            pltpu.VMEM((both, tasks), B16),
            pltpu.VMEM((2, in_width, hid), B16),
            pltpu.VMEM((2, hid, hid), B16),
            pltpu.VMEM((2, hid, LANES), B16),
            pltpu.VMEM((2, hid, bin_count), B16),
            pltpu.VMEM((in_width, hid), B16),
            pltpu.VMEM((hid, hid), B16),
            pltpu.VMEM((hid, lat), B16),
            pltpu.VMEM((6, 8, hid), F32),
            pltpu.VMEM((8, LANES), F32),
            pltpu.VMEM((lat, lat), B16),
            pltpu.VMEM((both, in_width), F32),
            q_wide, q_wide, q_wide, q_wide,
            pltpu.VMEM((both, LANES), B16),
            part_low, part_low, part_low, part_low, part_thin, pltpu.VMEM((QROWS, hid), F32),
            wide, wide, wide, wide,
            wide, wide, wide, wide, thin,
            full, full, low, low, low, low, low, low, low,
            pltpu.VMEM((2, CHIPS, block0, LANES), B16),
            pltpu.VMEM((3, CHIPS, block, LANES), B16),
            pltpu.VMEM((CHIPS, block0, LANES), B16),
            pltpu.VMEM((4, 48, hid), F32),
            pltpu.VMEM((24, LANES), F32),
            pltpu.VMEM((24, lat), F32),
            pltpu.VMEM((16, lat), F32),
            pltpu.VMEM((small_rows, LANES), F32),
            pltpu.VMEM((PEERS, small_rows, LANES), F32),
            pltpu.VMEM((steps, tasks, LANES), F32),
            dma((14,)), dma((chunks,)), dma((2 * chunks + 1,)),
            dma((chunks,)), dma((chunks,)), dma((chunks,)), dma((chunks,)),
            dma((2,)), dma((2,)), dma((chunks,)), dma((chunks,)), dma((chunks,)), dma((chunks,)),
            dma((4, CHIPS)), dma((4, CHIPS)), dma((4,)), dma((4, CHIPS)), dma((4, CHIPS)),
            dma((PEERS,)), dma((PEERS,)), dma((steps,)), dma((steps,)),
        ],
        compiler_params=pltpu.CompilerParams(
            collective_id=0, has_side_effects=True, vmem_limit_bytes=63 * 2**20
        ),
        name="step",
    )(
        latent_in, actions[0], meta, action_mask, table, latent_cot[0],
        w_in[0], w_mid[0], w_dyn_out[0], w_q_out[0],
        b_in[0], g_in[0], beta_in[0], b_mid[0], g_mid[0], beta_mid[0],
        b_dyn_out, g_dyn_out, beta_dyn_out, b_q_out[0],
    )
    q_parts = recv_q.astype(F32)
    shared = q_parts[0].sum(0)
    outer = q_parts[1:, 0] + q_parts[1:, 3]
    inner = q_parts[1:, 1] + q_parts[1:, 2]
    q_sum = jnp.stack([outer[0], outer[1], shared, inner[0], inner[1]])
    dyn_sum = recv_0.astype(F32).sum(0)

    across = [[q * PEERS + r for q in range(groups)] for r in range(PEERS)]

    def owned(piece, dim):
        if groups == 1:
            return piece
        piece = lax.psum_scatter(piece, "dp", scatter_dimension=dim, axis_index_groups=across, tiled=True)
        moves = [(q * PEERS + r, r * groups + q) for q in range(groups) for r in range(PEERS)]
        return lax.ppermute(piece, "dp", moves)

    part_in = owned(jnp.concatenate([dyn_sum[None, :in_width], q_sum[:, :in_width]], 0), 2)
    part_mid = owned(
        jnp.concatenate([dyn_sum[None, in_width : in_width + hid], q_sum[:, in_width : in_width + hid]], 0), 2
    )
    part_dyn = dyn_sum[in_width + hid : in_width + hid + lat].reshape(lat // LANES, LANES, LANES)
    part_dyn = owned(part_dyn.transpose(1, 0, 2).reshape(LANES, lat), 0)
    part_q = owned(q_sum[:, in_width + hid : in_width + hid + LANES, :bin_count], 1)
    vecs = owned(jnp.concatenate([dyn_sum[None, block0 - VECS :], q_sum[:, block - VECS :]], 0), 2)
    if groups > 1:
        small = lax.psum(small, "dp", axis_index_groups=across)
    at_q = tasks + 3 * (lat // LANES)
    grad_table = small[:tasks, :emb]
    dyn_vecs = small[tasks:at_q].reshape(3, lat)
    q_bias = small[at_q : at_q + heads, :bin_count]
    stat = small[at_q + heads, :3]
    rms = jnp.sqrt(jnp.stack([stat[1] / stat[0], stat[2] / (stat[0] * lat)]))[None]
    return (
        lat_out[None],
        grad_out[None],
        part_in[None],
        vecs[None, :, 0],
        vecs[None, :, 1],
        vecs[None, :, 2],
        part_mid[None],
        vecs[None, :, 3],
        vecs[None, :, 4],
        vecs[None, :, 5],
        part_dyn[None],
        dyn_vecs[0:1],
        dyn_vecs[1:2],
        dyn_vecs[2:3],
        part_q[None],
        q_bias[None],
        grad_table,
        rms,
    )


def solution(mesh):
    placed = (
        P("dp", None),
        P("section", "dp", None),
        P("dp"),
        P("dp"),
        P(),
        P("section", "dp"),
        P("section", "dp"),
        P("section", "dp", None),
        P("section", None, None, None),
        P("section", None, None),
        P("section", None, None),
        P("section", None, None),
        P("section", None, None, None),
        P("section", None, None),
        P("section", None, None),
        P("section", None, None),
        P("section", None, None),
        P("section", None),
        P("section", None),
        P("section", None),
        P("section", None, None, None),
        P("section", None, None),
        P(),
    )
    return jax.shard_map(
        on_device,
        mesh=mesh,
        in_specs=placed,
        out_specs=(
            P("section", "dp", None),
            P("section", "dp", None),
            P("section", None, None, "dp"),
            P("section", None, "dp"),
            P("section", None, "dp"),
            P("section", None, "dp"),
            P("section", None, None, "dp"),
            P("section", None, "dp"),
            P("section", None, "dp"),
            P("section", None, "dp"),
            P("section", "dp", None),
            P("section", None),
            P("section", None),
            P("section", None),
            P("section", None, "dp", None),
            P("section", None, None),
            P(),
            P("section", None),
        ),
        check_vma=False,
    )
```

time: 1540 us -> 287 us (0.19)
  matrix products: 440 us -> 0 us
  waiting for transfers between devices: 348 us -> 0 us
  other arithmetic: 346 us -> 16.6 us
  Pallas kernels: 0 us -> 245 us
  local copies, waits for them, and re-layouts: 259 us -> 17.5 us
  blocking collectives: 62.7 us -> 0 us
  starting transfers between devices: 42.7 us -> 0 us
  between operations: 27.4 us -> 3.41 us
    dot_general x93 -> x0, matrix products: 440 us -> none  [the longest x7 119 us: on_device(): jnp.einsum('hri,hrj->jhi', first_act, second_low, preferred_element_type=...]
    reduce_scatter x1 -> x0, waiting for transfers between devices: 336 us -> none  [on_device(): lax.psum_scatter(jnp.concatenate(pieces, 1), 'dp', scatter_dimension=0, t...]
    pallas_call x0 -> x1, Pallas kernels: none -> 245 us  [on_device(): pl.pallas_call(functools.partial(step_kernel, dims), out_shape=[jax.Shape...]
    reduce_sum x105 -> x2, other arithmetic: 195 us -> 2.28 us  [the longest x1 2.07 us: on_device(): dyn_sum = recv_0.astype(F32).sum(0)]
    dynamic_update_slice x41 -> x0, other arithmetic: 112 us -> none  [put_block(): lax.dynamic_update_index_in_dim(buffer, jnp.where(active, update, old_val...]
    concatenate x1 -> x0, local copies, waits for them, and re-layouts: 105 us -> none  [on_device(): jnp.concatenate(pieces, 1)]
    dynamic_slice x43 -> x0, local copies, waits for them, and re-layouts: 84 us -> none  [the longest x42 81.9 us: put_block(): old_value = lax.dynamic_index_in_dim(buffer, slot_index, 0, keepdims=False)]
    psum x2 -> x0, blocking collectives: 62.7 us -> none  [the longest x1 48.9 us: on_device(): table_total = lax.psum(table_sum, ('section', 'dp'))]
  transfers between devices with their start and end apart: 13 -> 0, of which waited for: 6 -> 0; matrix products, arithmetic and copies ran while one was open for 16% -> 0% of each run, Pallas kernels for 0% -> 0%
where the time goes in v1:
time: 287 us; the launch traced here: 282 us
  Pallas kernels  245 us (85%)
  local copies, waits for them, and re-layouts  17.5 us (6%)
  other arithmetic  16.6 us (6%)
  between operations  3.41 us (1%)
    pallas_call x1, Pallas kernels, on_device(): pl.pallas_call(functools.partial(step_kernel, dims), out_shape=[jax.Shape...  245 us
    unnamed x15, local copies, waits for them, and re-layouts  9.72 us

profile of v1, /device:TPU:14, one launch (start us, length us, event | category | flops | bytes accessed | tf_op | source)
XLA Modules:
  0.0 282.5 jit_solution(882756269331325097)
XLA Ops:
  0.7 0.7 convert_element_type.27
  1.3 0.7 convert_element_type.28
  2.0 0.7 convert_bitcast_fusion
  2.7 0.7 pad_maximum_fusion.1
  3.4 1.5 copy.64.refs_3_
  4.9 1.6 copy.61
  6.5 0.1 copy.62
  6.6 0.7 pad.4.refs_2_
  7.3 2.4 copy.63
  9.8 245.0 %step.1 = (bf16[512,512]{1,0:T(8,128)(2,1)}, f32[512,512]{1,0:T(8,128)}, bf16[3,4,1840,128]{3,2,1,0:T(8,128)(2,1)}, bf16[4,2224,128]{2,1,0:T(8,128)(2,1)}, f32[104,128]{1,0:T(8,128)}) custom-call(bf16[512,512]{1,0:T(8,128)(2,1)} %refs_0_.1, bf16[512,64]{1,0:T(8,128)(2,1)} %bitcast.77, f32[512,128]{1,0:T(8,128)} %pad.4.refs_2_, s32[80,64]{1,0:T(8,128)} %copy.64.refs_3_, ...), custom_call_target="tpu_custom_call" | custom-call | tf_op jit(solution)/shard_map/step/pallas_call | solution.py:664
  254.8 1.4 fusion.4
  258.9 0.6 maximum_sqrt_fusion
  259.4 0.7 slice_bitcast_fusion.5
  260.1 0.6 copy.69
  260.7 1.3 fusion.5
  262.1 1.4 slice.134
  263.5 2.1 convert_reduce_fusion
  265.6 0.2 copy.67
  265.8 0.8 broadcast_in_dim_reshape.3
  266.6 0.8 slice_bitcast_fusion.3
  267.4 3.3 %convert_element_type.32 = f32[3,4,1840,128]{3,2,1,0:T(8,128)S(1)} convert(bf16[3,4,1840,128]{3,2,1,0:T(8,128)(2,1)} %get-tuple-element.26) | non-fusion elementwise | flops 2826240 | bytes 16957440 | tf_op jit(solution)/shard_map/convert_element_type | solution.py:725
  270.7 0.2 slice_reduce_fusion
  270.9 0.2 fusion
  271.1 0.2 fusion.2
  271.3 0.0 copy-start
  271.3 0.6 maximum_bitcast_fusion.6
  271.9 0.6 fusion.3
  272.5 0.0 copy-done
  272.5 0.8 maximum_bitcast_fusion.2
  273.3 1.8 copy.68
  275.1 1.9 pad_maximum_fusion
  277.0 0.1 slice.144
  277.1 0.2 slice.147
  277.3 0.0 copy-start.1
  277.3 1.9 maximum_bitcast_fusion
  279.3 0.0 copy-done.1
  279.3 0.0 copy-start.3
  279.3 0.0 copy-start.2
  279.3 1.4 maximum_bitcast_fusion.1
  280.7 0.0 copy-done.3
  280.7 0.8 copy.74
  281.5 0.0 copy-done.2
  281.5 1.0 copy.75
  (3 shorter events, 0.1 us)
Async XLA Ops:
  271.3 1.3 copy-start
  277.3 1.9 copy-start.1
  279.3 1.4 copy-start.3
  279.3 2.2 copy-start.2

commit v2 on v1

v2 whole, which is shorter than its diff:
```python
import functools

import jax
import jax.numpy as jnp
from jax import lax
from jax.experimental import pallas as pl
from jax.experimental.pallas import tpu as pltpu
from jax.sharding import PartitionSpec as P

GROUP = 8
EPS = 1e-05
F32 = jnp.float32
B16 = jnp.bfloat16
MESH = pl.DeviceIdType.MESH

LANES = 128
CHIPS = 4
PEERS = 2 * CHIPS
CHUNK = 128
QROWS = 256
SUB = 256
VECS = 16

NN = (((1,), (0,)), ((), ()))
NT = (((1,), (1,)), ((), ()))
TN = (((0,), (0,)), ((), ()))


def dot(a, b, dims=NN):
    return lax.dot_general(a, b, dims, preferred_element_type=F32)


def split_dot(a, b, dims=NN):
    high = a.astype(B16)
    low = (a - high.astype(F32)).astype(B16)
    return dot(high, b, dims) + dot(low, b, dims)


def split_dot_right(a, b, dims):
    high = b.astype(B16)
    low = (b - high.astype(F32)).astype(B16)
    return dot(a, high, dims) + dot(a, low, dims)


def norm_mish(x, gain, shift):
    center = x - jnp.mean(x, -1, keepdims=True)
    spread = jnp.mean(center * center, -1, keepdims=True)
    scale = lax.rsqrt(spread + EPS)
    n = center * scale
    u = n * gain + shift
    w = jnp.exp(jnp.minimum(u, 30.0))
    top = w * (w + 2.0)
    over = pltpu.reciprocal(top + 2.0, approx=True)
    act = u * (top * over)
    slope = (top + 4.0 * (u * (top - w)) * over) * over
    return act, n, slope, scale


def tiles(size, step=256):
    return [(lo, min(lo + step, size)) for lo in range(0, size, step)]


def eight_rows(x):
    return x.reshape(x.shape[0] // 8, 8, x.shape[1]).sum(0)


def each_sub(count, body):
    if count <= SUB:
        body(0, count)
        return

    def step(j, carry):
        body(pl.multiple_of(j * SUB, SUB), SUB)
        return carry

    lax.fori_loop(0, count // SUB, step, 0)


def layer_forward(pre, count, bias, gain, shift, act_ref, act_at, n_ref, slope_ref, scale_ref, lane, at):
    def body(j, sub):
        act, n, slope, scale = norm_mish(pre[pl.ds(j, sub), :] + bias, gain, shift)
        act_ref[pl.ds(act_at + j, sub), :] = act.astype(B16)
        here = pl.ds(at + j, sub)
        n_ref[here, :] = n.astype(n_ref.dtype)
        slope_ref[here, :] = slope.astype(slope_ref.dtype)
        scale_ref[here, lane : lane + 1] = scale

    each_sub(count, body)


def layer_backward(pre, count, gain, n_ref, slope_ref, scale_ref, lane, at, out_ref, out_at, sums, first):
    def body(j, sub):
        here = pl.ds(at + j, sub)
        n = n_ref[here, :].astype(F32)
        du = pre[pl.ds(j, sub), :] * slope_ref[here, :].astype(F32)
        by_n = du * n
        dn = du * gain
        mean_dn = jnp.mean(dn, -1, keepdims=True)
        mean_by_n = jnp.mean(by_n * gain, -1, keepdims=True)
        out = (dn - mean_dn - n * mean_by_n) * scale_ref[here, lane : lane + 1]
        out_ref[pl.ds(out_at + j, sub), :] = out.astype(B16)
        sums[first : first + 8, :] += eight_rows(out)
        sums[first + 8 : first + 16, :] += eight_rows(by_n)
        sums[first + 16 : first + 24, :] += eight_rows(du)

    each_sub(count, body)


def step_kernel(dims, *refs):
    rows, lat, act_width, in_width, hid, heads, bins, tasks, emb, steps = dims
    side_width = in_width - lat
    block = in_width + hid + LANES + VECS
    block0 = in_width + hid + lat + VECS
    at_mid = in_width
    at_out = in_width + hid
    both = 2 * rows
    (
        lat_in, acts, task, valid, bin_at, part_of, amask, table, cot_in, w_in, w_mid, w_dyn, w_q,
        b_in, g_in, s_in, b_mid, g_mid, s_mid, b_dyn, g_dyn, s_dyn, b_q,
        lat_out, grad_out, recv_q, recv_0, small_out,
        x, m, wi, wm, wq, wq_raw, wi0, wm0, wd, vec, bq, diag,
        ig, act1, act2, spg, fpg, qg, n1, d1, n2, d2, q_scales, pre,
        act1_0, act2_0, spg_0, fpg_0, n1_0, d1_0, n2_0, d2_0, scales,
        dyn_n, new_lat, lat_low, cot, arrived, pair_grad, pair_send,
        gb, half_q, half_0, sums, q_sums, dyn_sums, stat, small, small_recv, table_recv,
        w_sem, in_sem, out_sem, lat_s, lat_r, px_s, px_r, side_s, side_r, pg_s, pg_r, gr_s, gr_r,
        half_s, half_r, own_s, rb_s, rb_r, sm_s, sm_r, tb_s, tb_r, up_s, up_r, dn_s, dn_r, up_ok, dn_ok,
    ) = refs
    section = lax.axis_index("section")
    d = lax.axis_index("dp")
    place = lax.rem(d, PEERS)
    base = d - place
    chip = place // 2
    core = lax.rem(place, 2)
    edge = (chip == 0) | (chip == CHIPS - 1)
    lower = chip < CHIPS // 2
    side_of = chip // 2
    last = steps - 1
    mate = base + chip * 2 + (1 - core)
    pair = base + (chip + 1 - 2 * lax.rem(chip, 2)) * 2 + core
    following = jnp.minimum(section + 1, last)
    before = jnp.maximum(section - 1, 0)
    chunks = rows // CHUNK
    jobs = jnp.where(edge, 2, 3)
    first_head = jnp.where(edge, 1, 3)

    def remote(src, dst, send, recv, to):
        return pltpu.make_async_remote_copy(
            src_ref=src, dst_ref=dst, send_sem=send, recv_sem=recv, device_id=to, device_id_type=MESH
        )

    def chunk_at(i):
        return pl.multiple_of(i * CHUNK, CHUNK)

    loads = [
        pltpu.make_async_copy(w_in.at[0], wi0, w_sem.at[0]),
        pltpu.make_async_copy(w_mid.at[0], wm0, w_sem.at[1]),
        pltpu.make_async_copy(w_dyn, wd, w_sem.at[2]),
    ]

    def job_loads(job):
        slot = lax.rem(job, 2)
        h = first_head + job
        return [
            pltpu.make_async_copy(w_in.at[h], wi.at[slot], w_sem.at[3 + 3 * slot]),
            pltpu.make_async_copy(w_mid.at[h], wm.at[slot], w_sem.at[4 + 3 * slot]),
            pltpu.make_async_copy(w_q.at[h - 1], wq_raw.at[slot], w_sem.at[5 + 3 * slot]),
        ]

    load_cot = pltpu.make_async_copy(cot_in, cot, w_sem.at[9])

    def load_lat(i):
        here = pl.ds(chunk_at(i), CHUNK)
        return pltpu.make_async_copy(lat_in.at[here], x.at[here, 0:lat], in_sem.at[i])

    loads[0].start()

    @pl.when(section == 0)
    def _():
        for i in range(chunks):
            load_lat(i).start()

    for copy in loads[1:] + job_loads(jnp.int32(0)) + job_loads(jnp.int32(1)):
        copy.start()
    load_cot.start()

    barrier = pltpu.get_barrier_semaphore()
    for other in range(1, PEERS):
        to = base + lax.rem(place + other, PEERS)
        pl.semaphore_signal(barrier, inc=1, device_id=(section, to), device_id_type=MESH)
    for other in range(1, steps):
        to = lax.rem(section + other, steps)
        pl.semaphore_signal(barrier, inc=1, device_id=(to, d), device_id_type=MESH)

    lines = [task[...].astype(F32), valid[...].astype(F32), bin_at[...].astype(F32), part_of[...]]
    lines.append(jnp.zeros((4, rows), F32))
    m[0:rows, 0:8] = jnp.concatenate(lines, 0).T

    def one_hot(lo, count):
        task_lane = lax.broadcasted_iota(jnp.int32, (count, tasks), 1).astype(F32)
        return (m[lo : lo + count, 0:1] == task_lane).astype(F32).astype(B16)

    hot = one_hot(0, rows)
    mask = dot(amask[...].astype(F32).astype(B16), hot, NT)
    acting = (acts[...].astype(F32) * mask).T
    side = jnp.concatenate([acting.astype(B16), dot(hot, table[...]).astype(B16)], 1)
    x[0:rows, lat:in_width] = side
    for t, source in enumerate((b_in, g_in, s_in, b_mid, g_mid, s_mid)):
        vec[t, 0 : heads + 1, :] = source[...].astype(F32)
    bq[...] = jnp.full(bq.shape, -1e30, F32)
    bq[0:heads, 0:bins] = b_q[...].astype(F32)
    wq[...] = jnp.zeros(wq.shape, B16)
    shift = GROUP.bit_length() - 1
    diag[...] = (
        lax.shift_right_logical(lax.broadcasted_iota(jnp.int32, (lat, lat), 0), shift)
        == lax.shift_right_logical(lax.broadcasted_iota(jnp.int32, (lat, lat), 1), shift)
    ).astype(F32).astype(B16)
    sums[...] = jnp.zeros(sums.shape, F32)
    ig[...] = jnp.zeros(ig.shape, F32)
    q_sums[...] = jnp.zeros(q_sums.shape, F32)
    dyn_sums[...] = jnp.zeros(dyn_sums.shape, F32)
    stat[...] = jnp.zeros(stat.shape, F32)
    small[...] = jnp.zeros(small.shape, F32)

    @pl.when(section == last)
    def _():
        arrived[...] = jnp.zeros(arrived.shape, B16)

    pl.semaphore_wait(barrier, PEERS - 1 + steps - 1)

    side_copy = remote(
        x.at[0:rows, lat : lat + 2 * LANES], x.at[rows:both, lat : lat + 2 * LANES],
        side_s.at[0], side_r.at[0], (section, pair),
    )
    meta_copy = remote(m.at[0:rows], m.at[rows:both], side_s.at[1], side_r.at[1], (section, pair))
    side_copy.start()
    meta_copy.start()
    for copy in loads:
        copy.wait()

    def vec_of(t, h):
        return vec[t, pl.ds(h, 1), :]

    def lat_copy(i):
        here = pl.ds(chunk_at(i), CHUNK)
        return remote(
            lat_low.at[here], x.at[here, 0:lat], lat_s.at[i], lat_r.at[i], (following, d)
        )

    def pair_copy(i):
        here = chunk_at(i)
        return remote(
            x.at[pl.ds(here, CHUNK), 0:lat], x.at[pl.ds(rows + here, CHUNK), 0:lat],
            px_s.at[i], px_r.at[i], (section, pair),
        )

    def lat_store(i):
        here = pl.ds(chunk_at(i), CHUNK)
        return pltpu.make_async_copy(lat_low.at[here], lat_out.at[here], out_sem.at[i])

    def forward_chunk(i, carry):
        at = chunk_at(i)
        here = pl.ds(at, CHUNK)

        @pl.when(section > 0)
        def _():
            lat_copy(i).wait_recv()

        @pl.when(section == 0)
        def _():
            load_lat(i).wait()

        pair_copy(i).start()
        pre[0:CHUNK, :] = dot(x[here, 0:in_width], wi0[...])
        layer_forward(
            pre, CHUNK, vec[0, 0:1, :], vec[1, 0:1, :], vec[2, 0:1, :], act1_0, at, n1_0, d1_0, scales, 0, at
        )
        pre[0:CHUNK, :] = dot(act1_0[here, :], wm0[...])
        layer_forward(
            pre, CHUNK, vec[3, 0:1, :], vec[4, 0:1, :], vec[5, 0:1, :], act2_0, at, n2_0, d2_0, scales, 1, at
        )
        out = dot(act2_0[here, :], wd[...]) + b_dyn[...].astype(F32)
        center = out - jnp.mean(out, -1, keepdims=True)
        scale = lax.rsqrt(jnp.mean(center * center, -1, keepdims=True) + EPS)
        normal = center * scale
        dyn_n[here, :] = normal.astype(B16)
        scales[here, 2:3] = scale
        power = jnp.exp(normal * g_dyn[...].astype(F32) + s_dyn[...].astype(F32))
        fresh = power * pltpu.reciprocal(split_dot(power, diag[...]), approx=True)
        new_lat[here, :] = fresh
        low = fresh.astype(B16)
        lat_low[here, :] = low

        @pl.when(section < last)
        def _():
            lat_copy(i).start()

        lat_store(i).start()
        wide = low.astype(F32)
        stat[0:8, :] += eight_rows(m[here, 1:2] * (wide * wide))
        return carry

    lax.fori_loop(0, chunks, forward_chunk, 0)

    def pg_copy(i):
        here = pl.ds(chunk_at(i), CHUNK)
        return remote(
            pair_send.at[here], pair_grad.at[here], pg_s.at[i], pg_r.at[i], (section, pair)
        )

    def q_chunk(job, at):
        here = pl.ds(at, QROWS)
        h = first_head + job
        slot = lax.rem(job, 2)
        pre[...] = dot(x[here, 0:in_width], wi[slot])
        layer_forward(
            pre, QROWS, vec_of(0, h), vec_of(1, h), vec_of(2, h), act1, at, n1, d1, q_scales, 0, 0
        )
        pre[...] = dot(act1[here, :], wm[slot])
        layer_forward(
            pre, QROWS, vec_of(3, h), vec_of(4, h), vec_of(5, h), act2, at, n2, d2, q_scales, 1, 0
        )
        logits = dot(act2[here, :], wq[slot], NT) + bq[pl.ds(h - 1, 1), :]
        power = jnp.exp(logits - jnp.max(logits, -1, keepdims=True))
        chance = power / jnp.sum(power, -1, keepdims=True)
        lane = lax.broadcasted_iota(jnp.int32, (QROWS, LANES), 1).astype(F32)
        low_bin = m[here, 2:3]
        part = m[here, 3:4]
        target = jnp.where(lane == low_bin, 1.0 - part, 0.0) + jnp.where(lane == low_bin + 1.0, part, 0.0)
        grad = (m[here, 1:2] * (chance - target)).astype(B16)
        qg[here, :] = grad
        q_sums[job] += eight_rows(grad.astype(F32))
        pre[...] = dot(grad, wq[slot])
        layer_backward(pre, QROWS, vec_of(4, h), n2, d2, q_scales, 1, 0, spg, at, sums.at[0], 24)
        pre[...] = dot(spg[here, :], wm[slot], NT)
        layer_backward(pre, QROWS, vec_of(1, h), n1, d1, q_scales, 0, 0, fpg, at, sums.at[0], 0)
        for lo, hi in tiles(in_width):
            ig[here, lo:hi] += dot(fpg[here, :], wi[slot, lo:hi, :], NT)

    q_chunks = both // QROWS
    own_chunks = rows // QROWS

    def q_job(job):
        for copy in job_loads(job):
            copy.wait()
        slot = lax.rem(job, 2)
        wq[slot, 0:bins, :] = wq_raw[slot]
        sums[0] = jnp.zeros(sums.shape[1:], F32)

        def body(i, carry):
            which = lax.rem(i + jnp.where(job == 0, 0, own_chunks), q_chunks)
            at = pl.multiple_of(which * QROWS, QROWS)

            @pl.when((job == 0) & (which == own_chunks))
            def _():
                side_copy.wait_recv()
                meta_copy.wait_recv()

                def pair_here(j, carry):
                    pair_copy(j).wait_recv()
                    return carry

                lax.fori_loop(0, chunks, pair_here, 0)

            q_chunk(job, at)

            @pl.when((job == jobs - 1) & (which >= own_chunks))
            def _():
                for k in range(QROWS // CHUNK):
                    j = (which - own_chunks) * (QROWS // CHUNK) + k
                    to = chunk_at(j)
                    pair_send[pl.ds(to, CHUNK), :] = ig[pl.ds(rows + to, CHUNK), 0:lat].astype(B16)
                    pg_copy(j).start()

            return carry

        lax.fori_loop(0, q_chunks, body, 0)

        @pl.when(job + 2 < jobs)
        def _():
            for copy in job_loads(job + 2):
                copy.start()

    def half_copy(job, z, q):
        if q:
            src, dst = gb.at[1 - core, z, 0:block], half_q.at[job, z]
        else:
            src, dst = gb.at[1 - core, z], half_0.at[z]
        return remote(src, dst, half_s.at[job, z], half_r.at[job, z], (section, mate))

    def owner_copy(job, z):
        head = first_head + job - 1
        return remote(
            half_q.at[job, z], recv_q.at[head, side_of], rb_s.at[job, z], rb_r.at[head, side_of],
            (section, base + 2 * z + core),
        )

    def keep_copy(job):
        return pltpu.make_async_copy(
            half_q.at[job, chip], recv_q.at[first_head + job - 1, side_of], own_s.at[job]
        )

    def add_rows(dst, src, size):
        step = size // 4 // 16 * 16
        for part in range(4):
            span = slice(part * step, size if part == 3 else (part + 1) * step)
            dst[span, :] = (dst[span, :].astype(F32) + src[span, :].astype(F32)).astype(B16)

    def weight_grads(job, q):
        if q:
            count, a1, a2, sp, fp, own_sums = both, act1, act2, spg, fpg, 0
        else:
            count, a1, a2, sp, fp, own_sums = rows, act1_0, act2_0, spg_0, fpg_0, 1
        size = block if q else block0

        def order(i):
            return jnp.where(lower, CHIPS - 1 - i, i)

        def make(z):
            cols = pl.ds(pl.multiple_of(z * 2 * LANES, 2 * LANES), 2 * LANES)
            for left, right, first, size_of in ((x, fp, 0, in_width), (a1, sp, at_mid, hid)):
                for lo, hi in tiles(size_of):
                    grad = dot(left[0:count, lo:hi], right[0:count, cols], TN)
                    for p in range(2):
                        gb[p, z, first + lo : first + hi, :] = grad[:, p * LANES : (p + 1) * LANES].astype(B16)
            if q:
                g_out = dot(qg[0:count, :], a2[0:count, cols], TN)
                for p in range(2):
                    gb[p, z, at_out : at_out + LANES, :] = g_out[:, p * LANES : (p + 1) * LANES].astype(B16)
            else:
                g_out = dot(a2[0:count, cols], arrived[0:count, :], TN)
                for p in range(2):
                    for t in range(lat // LANES):
                        gb[p, z, at_out + t * LANES : at_out + (t + 1) * LANES, :] = g_out[
                            p * LANES : (p + 1) * LANES, t * LANES : (t + 1) * LANES
                        ].astype(B16)
            lines = [jnp.sum(sums[own_sums, 8 * t : 8 * t + 8, cols], 0, keepdims=True) for t in range(6)]
            lines.append(jnp.zeros((VECS - 6, 2 * LANES), F32))
            vectors = jnp.concatenate(lines, 0).astype(B16)
            for p in range(2):
                gb[p, z, size - VECS : size, :] = vectors[:, p * LANES : (p + 1) * LANES]
            half_copy(job, z, q).start()

        def finish(z):
            half_copy(job, z, q).wait_recv()
            if q:
                add_rows(half_q.at[job, z], gb.at[core, z], size)

                @pl.when(z != chip)
                def _():
                    owner_copy(job, z).start()

                @pl.when(z == chip)
                def _():
                    keep_copy(job).start()
            else:
                add_rows(half_0.at[z], gb.at[core, z], size)

        def body(i, carry):
            @pl.when(i < CHIPS)
            def _():
                make(order(i))

            @pl.when(i > 0)
            def _():
                finish(order(i - 1))

            return carry

        lax.fori_loop(0, CHIPS + 1, body, 0)

        def sent(z, carry):
            half_copy(job, z, q).wait_send()
            return carry

        lax.fori_loop(0, CHIPS, sent, 0)

    def job_body(job, carry):
        q_job(job)

        @pl.when(job < jobs - 1)
        def _():
            weight_grads(job, True)

        return carry

    lax.fori_loop(0, jobs, job_body, 0)

    def back_copy(i):
        here = pl.ds(chunk_at(i), CHUNK)
        return remote(lat_low.at[here], arrived.at[here], gr_s.at[i], gr_r.at[i], (before, d))

    def grad_store(i):
        here = pl.ds(chunk_at(i), CHUNK)
        return pltpu.make_async_copy(ig.at[here, 0:lat], grad_out.at[here], out_sem.at[chunks + i])

    def lat_sent(i, carry):
        lat_store(i).wait()

        @pl.when(section < last)
        def _():
            lat_copy(i).wait_send()

        return carry

    def backward_chunk(i, carry):
        at = chunk_at(i)
        here = pl.ds(at, CHUNK)

        @pl.when(section < last)
        def _():
            back_copy(i).wait_recv()

        out_grad = cot[here, :].astype(F32) + arrived[here, :].astype(F32)
        fresh = new_lat[here, :]
        normal = dyn_n[here, :].astype(F32)
        norm_grad = fresh * (out_grad - split_dot(out_grad * fresh, diag[...]))
        by_n = norm_grad * normal
        gain = g_dyn[...].astype(F32)
        dm = norm_grad * gain
        mean_dm = jnp.mean(dm, -1, keepdims=True)
        mean_by_n = jnp.mean(by_n * gain, -1, keepdims=True)
        low = ((dm - mean_dm - normal * mean_by_n) * scales[here, 2:3]).astype(B16)
        arrived[here, :] = low
        dyn_sums[0:8, :] += eight_rows(low.astype(F32))
        dyn_sums[8:16, :] += eight_rows(by_n)
        dyn_sums[16:24, :] += eight_rows(norm_grad)
        pre[0:CHUNK, :] = dot(low, wd[...], NT)
        layer_backward(pre, CHUNK, vec[4, 0:1, :], n2_0, d2_0, scales, 1, at, spg_0, at, sums.at[1], 24)
        pre[0:CHUNK, :] = dot(spg_0[here, :], wm0[...], NT)
        layer_backward(pre, CHUNK, vec[1, 0:1, :], n1_0, d1_0, scales, 0, at, fpg_0, at, sums.at[1], 0)
        back_in = dot(fpg_0[here, :], wi0[...], NT)
        pg_copy(i).wait_recv()
        total = back_in[:, 0:lat] + ig[here, 0:lat] + pair_grad[here, :].astype(F32)
        lat_low[here, :] = total.astype(B16)

        @pl.when(section > 0)
        def _():
            back_copy(i).start()

        ig[here, 0:lat] = total
        grad_store(i).start()
        stat[8:16, :] += eight_rows(m[here, 1:2] * (total * total))
        ig[here, lat:in_width] += back_in[:, lat:in_width]
        return carry

    def small_copy(other):
        to = base + lax.rem(place + other, PEERS)
        return remote(small, small_recv.at[place], sm_s.at[other], sm_r.at[place], (section, to))

    def small_arrival(other):
        source = lax.rem(place + other, PEERS)
        return remote(small, small_recv.at[source], sm_s.at[other], sm_r.at[source], (section, base + source))

    def send_small():
        table_part = jnp.zeros((tasks, side_width), F32)
        for lo in (0, rows):
            table_part += split_dot_right(one_hot(lo, rows), ig[lo : lo + rows, lat:in_width], TN)
        small[0:tasks, 0:emb] = table_part[:, side_width - emb :]
        for t in range(3):
            line = jnp.sum(dyn_sums[8 * t : 8 * t + 8, :], 0, keepdims=True)
            for part in range(lat // LANES):
                row = tasks + t * (lat // LANES) + part
                small[row : row + 1, :] = line[:, part * LANES : (part + 1) * LANES]
        q_lines = [jnp.sum(q_sums[job], 0, keepdims=True) for job in range(3)]
        for h in range(heads):
            line = jnp.zeros((1, LANES), F32)
            for job in range(3):
                line += jnp.where(first_head + job == h + 1, q_lines[job], 0.0)
            row = tasks + 3 * (lat // LANES) + h
            small[row : row + 1, :] = line
        row = tasks + 3 * (lat // LANES) + heads
        lane = lax.broadcasted_iota(jnp.int32, (1, LANES), 1)
        count = jnp.sum(m[0:rows, 1:2], 0, keepdims=True)
        lat_square = jnp.sum(jnp.sum(stat[0:8, :], 0, keepdims=True), 1, keepdims=True)
        grad_square = jnp.sum(jnp.sum(stat[8:16, :], 0, keepdims=True), 1, keepdims=True)
        small[row : row + 1, :] = jnp.where(
            lane == 0, count, jnp.where(lane == 1, lat_square, jnp.where(lane == 2, grad_square, 0.0))
        )
        small_recv[place] = small[...]
        for other in range(1, PEERS):
            small_copy(other).start()

    load_cot.wait()
    lax.fori_loop(0, chunks, lat_sent, 0)

    def late(turn, carry):
        @pl.when((turn == 0) == (section == last))
        def _():
            lax.fori_loop(0, chunks, backward_chunk, 0)
            send_small()

        @pl.when((turn == 0) == (section < last))
        def _():
            weight_grads(jobs - 1, True)

        return carry

    lax.fori_loop(0, 2, late, 0)
    weight_grads(jnp.int32(3), False)

    def at_chip(z):
        return (section, base + 2 * z + core)

    def up_copy(t):
        return remote(half_0.at[t], gb.at[0, t], up_s.at[t], up_r.at[t], at_chip(jnp.minimum(chip + 1, CHIPS - 1)))

    def down_copy(t):
        return remote(half_0.at[t], gb.at[1, t], dn_s.at[t], dn_r.at[t], at_chip(jnp.maximum(chip - 1, 0)))

    @pl.when(chip > 0)
    def _():
        pl.semaphore_signal(up_ok, inc=1, device_id=at_chip(jnp.maximum(chip - 1, 0)), device_id_type=MESH)

    @pl.when(chip < CHIPS - 1)
    def _():
        pl.semaphore_signal(
            dn_ok, inc=1, device_id=at_chip(jnp.minimum(chip + 1, CHIPS - 1)), device_id_type=MESH
        )

    def hops(turn, carry):
        @pl.when(((turn == 0) == lower) & (chip < CHIPS - 1))
        def _():
            pl.semaphore_wait(up_ok, 1)
            for t in range(CHIPS - 1, 0, -1):
                @pl.when(t > chip)
                def _():
                    @pl.when(chip > 0)
                    def _():
                        up_copy(t).wait_recv()
                        add_rows(half_0.at[t], gb.at[0, t], block0)

                    up_copy(t).start()

        @pl.when(((turn == 0) != lower) & (chip > 0))
        def _():
            pl.semaphore_wait(dn_ok, 1)
            for t in range(CHIPS - 1):
                @pl.when(t < chip)
                def _():
                    @pl.when(chip < CHIPS - 1)
                    def _():
                        down_copy(t).wait_recv()
                        add_rows(half_0.at[t], gb.at[1, t], block0)

                    down_copy(t).start()

        return carry

    lax.fori_loop(0, 2, hops, 0)

    for other in range(1, PEERS):
        small_arrival(other).wait_recv()
    total = small_recv[0]
    for source in range(1, PEERS):
        total = total + small_recv[source]
    for other in range(1, PEERS):
        small_copy(other).wait_send()
    small[...] = total
    table_recv[section] = small[0:tasks, :]

    def table_copy(other):
        to = lax.rem(section + other, steps)
        return remote(
            small.at[0:tasks], table_recv.at[section], tb_s.at[other], tb_r.at[section], (to, d)
        )

    def table_arrival(other):
        source = lax.rem(section + other, steps)
        return remote(small.at[0:tasks], table_recv.at[source], tb_s.at[other], tb_r.at[source], (source, d))

    for other in range(1, steps):
        table_copy(other).start()

    side_copy.wait_send()
    meta_copy.wait_send()

    def sends(i, carry):
        pair_copy(i).wait_send()
        pg_copy(i).wait_send()
        grad_store(i).wait()

        @pl.when(section > 0)
        def _():
            back_copy(i).wait_send()

        return carry

    lax.fori_loop(0, chunks, sends, 0)

    def job_done(job, carry):
        def body(other, carry):
            owner_copy(job, lax.rem(chip + other, CHIPS)).wait_send()
            return carry

        lax.fori_loop(1, CHIPS, body, 0)
        keep_copy(job).wait()
        return carry

    lax.fori_loop(0, jobs, job_done, 0)
    for head in range(heads):
        for half in range(2):
            source = (0, CHIPS - 1)[half] if head < 2 else (1, CHIPS - 2)[half]

            @pl.when(chip != source)
            def _():
                remote(
                    half_q.at[0, 0], recv_q.at[head, half], rb_s.at[0, 0], rb_r.at[head, half], at_chip(source)
                ).wait_recv()

    @pl.when(chip > 0)
    def _():
        up_copy(chip).wait_recv()
        add_rows(half_0.at[chip], gb.at[0, chip], block0)

    @pl.when(chip < CHIPS - 1)
    def _():
        down_copy(chip).wait_recv()
        add_rows(half_0.at[chip], gb.at[1, chip], block0)

    keep_0 = pltpu.make_async_copy(half_0.at[chip], recv_0, own_s.at[3])
    keep_0.start()
    for t in range(CHIPS):
        @pl.when(t > chip)
        def _():
            up_copy(t).wait_send()

        @pl.when(t < chip)
        def _():
            down_copy(t).wait_send()

    for other in range(1, steps):
        table_arrival(other).wait_recv()
    for other in range(1, steps):
        table_copy(other).wait_send()
    whole = table_recv[0]
    for source in range(1, steps):
        whole = whole + table_recv[source]
    small[0:tasks, :] = whole
    done = pltpu.make_async_copy(small, small_out, out_sem.at[2 * chunks])
    done.start()
    done.wait()
    keep_0.wait()


def finish_kernel(dims, *refs):
    lat, in_width, hid, heads, bins, tasks, emb = dims
    block = in_width + hid + LANES + VECS
    block0 = in_width + hid + lat + VECS
    at_out = in_width + hid
    recv_q, recv_0, small, lat_in, grad_in = refs[:5]
    lat_out, grad_out, w_in, w_mid, w_dyn, w_q, b_dyn, g_dyn, s_dyn, b_q, table, rms = refs[5:17]
    vecs = refs[17:23]
    sem = refs[23]
    copies = [
        pltpu.make_async_copy(lat_in, lat_out, sem.at[0]),
        pltpu.make_async_copy(grad_in, grad_out, sem.at[1]),
    ]
    for copy in copies:
        copy.start()

    def total(h, lo, hi):
        if h == 0:
            return recv_0[lo:hi, :].astype(F32)
        return recv_q[h - 1, 0, lo:hi, :].astype(F32) + recv_q[h - 1, 1, lo:hi, :].astype(F32)

    for h in range(heads + 1):
        w_in[h] = total(h, 0, in_width)
        w_mid[h] = total(h, in_width, at_out)
        size = block if h else block0
        lines = total(h, size - VECS, size)
        for t in range(6):
            vecs[t][h] = lines[t : t + 1, :]
        if h:
            w_q[h - 1] = total(h, at_out, at_out + LANES)[0:bins, :]
    for t in range(lat // LANES):
        w_dyn[:, t * LANES : (t + 1) * LANES] = total(0, at_out + t * LANES, at_out + (t + 1) * LANES)
    table[...] = small[0:tasks, 0:emb]
    for t, out in enumerate((b_dyn, g_dyn, s_dyn)):
        for part in range(lat // LANES):
            row = tasks + t * (lat // LANES) + part
            out[0:1, part * LANES : (part + 1) * LANES] = small[row : row + 1, :]
    at_q = tasks + 3 * (lat // LANES)
    for h in range(heads):
        b_q[h] = small[at_q + h : at_q + h + 1, 0:bins]
    stat = small[at_q + heads : at_q + heads + 1, :]
    count = stat[:, 0:1]
    squares = jnp.concatenate([stat[:, 1:2] / count, stat[:, 2:3] / (count * lat)], 1)
    rms[...] = jnp.sqrt(squares)
    for copy in copies:
        copy.wait()


def on_device(
    latent_in, actions, task_ids, valid, action_mask, bins, fraction, latent_cot,
    w_in, b_in, g_in, beta_in, w_mid, b_mid, g_mid, beta_mid,
    w_dyn_out, b_dyn_out, g_dyn_out, beta_dyn_out, w_q_out, b_q_out, table,
):
    steps = lax.axis_size("section")
    spread = lax.axis_size("dp")
    groups = spread // PEERS
    rows, lat = latent_in.shape
    act_width = actions.shape[2]
    in_width, hid = w_in.shape[2:]
    heads = w_q_out.shape[1]
    bin_count = w_q_out.shape[-1]
    tasks, emb = table.shape
    block = in_width + hid + LANES + VECS
    block0 = in_width + hid + lat + VECS
    chunks = rows // CHUNK
    small_rows = tasks + 24
    dims = (rows, lat, act_width, in_width, hid, heads, bin_count, tasks, emb, steps)
    anywhere = pl.BlockSpec(memory_space=pl.ANY)
    vmem = pl.BlockSpec(memory_space=pltpu.VMEM)
    dma = pltpu.SemaphoreType.DMA
    both = 2 * rows
    wide = pltpu.VMEM((rows, hid), B16)
    thin = pltpu.VMEM((rows, LANES), F32)
    low = pltpu.VMEM((rows, lat), B16)
    part_low = pltpu.VMEM((QROWS, hid), B16)
    q_wide = pltpu.VMEM((both, hid), B16)
    lat_out, grad_out, recv_q, recv_0, small = pl.pallas_call(
        functools.partial(step_kernel, dims),
        out_shape=[
            jax.ShapeDtypeStruct((rows, lat), B16),
            jax.ShapeDtypeStruct((rows, lat), F32),
            jax.ShapeDtypeStruct((heads, 2, block, LANES), B16),
            jax.ShapeDtypeStruct((block0, LANES), B16),
            jax.ShapeDtypeStruct((small_rows, LANES), F32),
        ],
        in_specs=[anywhere] + [vmem] * 7 + [anywhere] * 5 + [vmem] * 10,
        out_specs=[anywhere] * 5,
        scratch_shapes=[
            pltpu.VMEM((both, 6 * LANES), B16),
            pltpu.VMEM((both, LANES), F32),
            pltpu.VMEM((2, in_width, hid), B16),
            pltpu.VMEM((2, hid, hid), B16),
            pltpu.VMEM((2, LANES, hid), B16),
            pltpu.VMEM((2, bin_count, hid), B16),
            pltpu.VMEM((in_width, hid), B16),
            pltpu.VMEM((hid, hid), B16),
            pltpu.VMEM((hid, lat), B16),
            pltpu.VMEM((6, 8, hid), F32),
            pltpu.VMEM((8, LANES), F32),
            pltpu.VMEM((lat, lat), B16),
            pltpu.VMEM((both, in_width), F32),
            q_wide, q_wide, q_wide, q_wide,
            pltpu.VMEM((both, LANES), B16),
            part_low, part_low, part_low, part_low,
            pltpu.VMEM((QROWS, LANES), F32),
            pltpu.VMEM((QROWS, hid), F32),
            wide, wide, wide, wide, wide, wide, wide, wide, thin,
            low,
            pltpu.VMEM((rows, lat), F32),
            low, low, low, low, low,
            pltpu.VMEM((2, CHIPS, block0, LANES), B16),
            pltpu.VMEM((3, CHIPS, block, LANES), B16),
            pltpu.VMEM((CHIPS, block0, LANES), B16),
            pltpu.VMEM((2, 48, hid), F32),
            pltpu.VMEM((3, 8, LANES), F32),
            pltpu.VMEM((24, lat), F32),
            pltpu.VMEM((16, lat), F32),
            pltpu.VMEM((small_rows, LANES), F32),
            pltpu.VMEM((PEERS, small_rows, LANES), F32),
            pltpu.VMEM((steps, tasks, LANES), F32),
            dma((10,)), dma((chunks,)), dma((2 * chunks + 1,)),
            dma((chunks,)), dma((chunks,)), dma((chunks,)), dma((chunks,)),
            dma((2,)), dma((2,)), dma((chunks,)), dma((chunks,)), dma((chunks,)), dma((chunks,)),
            dma((4, CHIPS)), dma((4, CHIPS)), dma((4,)), dma((3, CHIPS)), dma((heads, 2)),
            dma((PEERS,)), dma((PEERS,)), dma((steps,)), dma((steps,)),
            dma((CHIPS,)), dma((CHIPS,)), dma((CHIPS,)), dma((CHIPS,)),
            pltpu.SemaphoreType.REGULAR, pltpu.SemaphoreType.REGULAR,
        ],
        compiler_params=pltpu.CompilerParams(
            collective_id=0, has_side_effects=True, vmem_limit_bytes=16350 * 2**12
        ),
        name="step",
    )(
        latent_in, actions[0].T, task_ids[None], valid[None], bins, fraction,
        action_mask.T, table, latent_cot[0],
        w_in[0], w_mid[0], w_dyn_out[0], w_q_out[0].transpose(0, 2, 1),
        b_in[0], g_in[0], beta_in[0], b_mid[0], g_mid[0], beta_mid[0],
        b_dyn_out, g_dyn_out, beta_dyn_out, b_q_out[0],
    )
    across = [[q * PEERS + r for q in range(groups)] for r in range(PEERS)]
    if groups > 1:
        small = lax.psum(small, "dp", axis_index_groups=across)

    def shape(*dims):
        return jax.ShapeDtypeStruct(dims, F32)

    lat_out, grad_out, part_in, part_mid, part_dyn, part_q, b_dyn, g_dyn, s_dyn, q_bias, grad_table, rms, *vecs = (
        pl.pallas_call(
            functools.partial(finish_kernel, (lat, in_width, hid, heads, bin_count, tasks, emb)),
            out_shape=[
                jax.ShapeDtypeStruct((rows, lat), B16),
                shape(rows, lat),
                shape(heads + 1, in_width, LANES),
                shape(heads + 1, hid, LANES),
                shape(LANES, lat),
                shape(heads, bin_count, LANES),
                shape(1, lat), shape(1, lat), shape(1, lat),
                shape(heads, 1, bin_count),
                shape(tasks, emb),
                shape(1, 2),
            ] + [shape(heads + 1, 1, LANES)] * 6,
            in_specs=[vmem] * 3 + [anywhere] * 2,
            out_specs=[anywhere] * 2 + [vmem] * 16,
            scratch_shapes=[dma((2,))],
            compiler_params=pltpu.CompilerParams(vmem_limit_bytes=40 * 2**20),
            name="finish",
        )(recv_q, recv_0, small, lat_out, grad_out)
    )

    def owned(piece, dim):
        if groups == 1:
            return piece
        piece = lax.psum_scatter(piece, "dp", scatter_dimension=dim, axis_index_groups=across, tiled=True)
        moves = [(q * PEERS + r, r * groups + q) for q in range(groups) for r in range(PEERS)]
        return lax.ppermute(piece, "dp", moves)

    part_in, part_mid, part_q = owned(part_in, 2), owned(part_mid, 2), owned(part_q, 2)
    part_dyn = owned(part_dyn, 0)
    vecs = [owned(v, 2).transpose(1, 0, 2) for v in vecs]
    return (
        lat_out[None],
        grad_out[None],
        part_in[None],
        *vecs[:3],
        part_mid[None],
        *vecs[3:],
        part_dyn[None],
        b_dyn,
        g_dyn,
        s_dyn,
        part_q.transpose(0, 2, 1)[None],
        q_bias.transpose(1, 0, 2),
        grad_table,
        rms,
    )


def solution(mesh):
    placed = (
        P("dp", None),
        P("section", "dp", None),
        P("dp"),
        P("dp"),
        P(),
        P("section", "dp"),
        P("section", "dp"),
        P("section", "dp", None),
        P("section", None, None, None),
        P("section", None, None),
        P("section", None, None),
        P("section", None, None),
        P("section", None, None, None),
        P("section", None, None),
        P("section", None, None),
        P("section", None, None),
        P("section", None, None),
        P("section", None),
        P("section", None),
        P("section", None),
        P("section", None, None, None),
        P("section", None, None),
        P(),
    )
    return jax.shard_map(
        on_device,
        mesh=mesh,
        in_specs=placed,
        out_specs=(
            P("section", "dp", None),
            P("section", "dp", None),
            P("section", None, None, "dp"),
            P("section", None, "dp"),
            P("section", None, "dp"),
            P("section", None, "dp"),
            P("section", None, None, "dp"),
            P("section", None, "dp"),
            P("section", None, "dp"),
            P("section", None, "dp"),
            P("section", "dp", None),
            P("section", None),
            P("section", None),
            P("section", None),
            P("section", None, "dp", None),
            P("section", None, None),
            P(),
            P("section", None),
        ),
        check_vma=False,
    )
```

time: 287 us -> 218 us (0.76); the launches traced: 282 us -> 218 us
  Pallas kernels: 245 us -> 210 us
  other arithmetic: 16.6 us -> 0 us
  local copies, waits for them, and re-layouts: 17.5 us -> 7.42 us
    pallas_call x1, Pallas kernels: 245 us -> 206 us  [on_device(): pl.pallas_call(functools.partial(step_kernel, dims), out_shape=[jax.Shape...]
    convert_element_type x4 -> x0, other arithmetic: 5.38 us -> none  [the longest x1 3.33 us: on_device(): q_parts = recv_q.astype(F32)]
    slice x6 -> x0, local copies, waits for them, and re-layouts: 4.42 us -> none  [the longest x1 1.4 us: on_device(): grad_table = small[:tasks, :emb]]
    broadcast_in_dim x3 -> x0, other arithmetic: 4.12 us -> none  [the longest x1 1.93 us: on_device(): part_mid[None]]
    another operation x4 -> x0, other arithmetic: 3.81 us -> none  [the longest x1 1.88 us: on_device(): q_sum = jnp.stack([outer[0], outer[1], shared, inner[0], inner[1]])]
    pallas_call x0 -> x1, Pallas kernels: none -> 3.7 us  [on_device(): pl.pallas_call(functools.partial(finish_kernel, (lat, in_width, hid, head...]
    unnamed x15 -> x11, local copies, waits for them, and re-layouts: 9.72 us -> 7.42 us
where the time goes in v2:
time: 218 us
  Pallas kernels  210 us (96%)
  local copies, waits for them, and re-layouts  7.42 us (3%)
    pallas_call x1, Pallas kernels, on_device(): pl.pallas_call(functools.partial(step_kernel, dims), out_shape=[jax.Shape...  206 us
    unnamed x11, local copies, waits for them, and re-layouts  7.42 us

profile of v2, /device:TPU:14, one launch (start us, length us, event | category | flops | bytes accessed | tf_op | source)
XLA Modules:
  0.0 218.0 jit_solution(17655700152463050599)
XLA Ops:
  0.7 206.2 %step.1 = (bf16[512,512]{1,0:T(8,128)(2,1)}, f32[512,512]{1,0:T(8,128)}, bf16[5,2,1840,128]{3,2,1,0:T(8,128)(2,1)}, bf16[2224,128]{1,0:T(8,128)(2,1)}, f32[104,128]{1,0:T(8,128)}) custom-call(bf16[512,512]{1,0:T(8,128)(2,1)} %refs_0_.1, bf16[64,512]{1,0:T(8,128)(2,1)} %bitcast.41, s32[1,512]{1,0:T(1,128)} %bitcast.49, s32[1,512]{1,0:T(1,128)} %bitcast.50, ...), custom_call_target="tpu_custom_call" | custom-call | tf_op jit(solution)/shard_map/step/pallas_call | solution.py:822
  206.8 0.0 copy-start
  206.8 2.3 %copy-done = bf16[5,2,1840,128]{3,2,1,0:T(8,128)(2,1)S(1)} copy-done((bf16[5,2,1840,128]{3,2,1,0:T(8,128)(2,1)S(1)}, bf16[5,2,1840,128]{3,2,1,0:T(8,128)(2,1)}, u32[]{:S(2)}) %copy-start) | copy-done | bytes 4710424
  209.2 0.0 copy-start.1
  209.2 1.2 copy-done.1
  210.4 0.0 copy-start.2
  210.4 1.1 copy-done.2
  211.4 0.0 copy-start.3
  211.4 1.0 copy-done.3
  212.5 0.0 copy-start.4
  212.5 0.8 copy-done.4
  213.3 3.7 %finish.1 = (bf16[512,512]{1,0:T(8,128)(2,1)}, f32[512,512]{1,0:T(8,128)}, f32[6,672,128]{2,1,0:T(8,128)}, f32[6,1024,128]{2,1,0:T(8,128)}, f32[128,512]{1,0:T(8...) custom-call(bf16[5,2,1840,128]{3,2,1,0:T(8,128)(2,1)S(1)} %copy-done, ...), custom_call_target="tpu_custom_call" | custom-call | tf_op jit(solution)/shard_map/finish/pallas_call | solution.py:893
  217.0 1.0 copy.41
Async XLA Ops:
  206.8 2.3 %copy-start = (bf16[5,2,1840,128]{3,2,1,0:T(8,128)(2,1)S(1)}, bf16[5,2,1840,128]{3,2,1,0:T(8,128)(2,1)}, u32[]{:S(2)}) copy-start(bf16[5,2,1840,128]{3,2,1,0:T(8,128)(2,1)} %get-tuple-element.41.refs_0_) | copy-start | bytes 14131204
  209.2 1.2 copy-start.1
  210.4 1.1 copy-start.2
  211.4 1.0 copy-start.3
  212.5 0.8 copy-start.4

commit v3 on v2

--- a/solution.py
+++ b/solution.py
@@ -52,8 +52,12 @@
     top = w * (w + 2.0)
     over = pltpu.reciprocal(top + 2.0, approx=True)
     act = u * (top * over)
-    slope = (top + 4.0 * (u * (top - w)) * over) * over
+    slope = (top + 4.0 * (u * (top - w)) * over) * (over * gain)
     return act, n, slope, scale
+
+
+def padded(count):
+    return (count + 15) // 16 * 16
 
 
 def tiles(size, step=256):
@@ -65,20 +69,17 @@
 
 
 def each_sub(count, body):
-    if count <= SUB:
-        body(0, count)
-        return
-
-    def step(j, carry):
-        body(pl.multiple_of(j * SUB, SUB), SUB)
-        return carry
-
-    lax.fori_loop(0, count // SUB, step, 0)
+    sub = min(SUB, count)
+    for j in range(0, count, sub):
+        body(j, sub)
 
 
 def layer_forward(pre, count, bias, gain, shift, act_ref, act_at, n_ref, slope_ref, scale_ref, lane, at):
     def body(j, sub):
-        act, n, slope, scale = norm_mish(pre[pl.ds(j, sub), :] + bias, gain, shift)
+        x = pre[pl.ds(j, sub), :]
+        if bias is not None:
+            x = x + bias
+        act, n, slope, scale = norm_mish(x, gain, shift)
         act_ref[pl.ds(act_at + j, sub), :] = act.astype(B16)
         here = pl.ds(at + j, sub)
         n_ref[here, :] = n.astype(n_ref.dtype)
@@ -88,20 +89,18 @@
     each_sub(count, body)
 
 
-def layer_backward(pre, count, gain, n_ref, slope_ref, scale_ref, lane, at, out_ref, out_at, sums, first):
+def layer_backward(pre, count, n_ref, slope_ref, scale_ref, lane, at, out_ref, out_at, sums, first):
     def body(j, sub):
         here = pl.ds(at + j, sub)
         n = n_ref[here, :].astype(F32)
-        du = pre[pl.ds(j, sub), :] * slope_ref[here, :].astype(F32)
-        by_n = du * n
-        dn = du * gain
+        dn = pre[pl.ds(j, sub), :] * slope_ref[here, :].astype(F32)
+        by_n = dn * n
         mean_dn = jnp.mean(dn, -1, keepdims=True)
-        mean_by_n = jnp.mean(by_n * gain, -1, keepdims=True)
+        mean_by_n = jnp.mean(by_n, -1, keepdims=True)
         out = (dn - mean_dn - n * mean_by_n) * scale_ref[here, lane : lane + 1]
         out_ref[pl.ds(out_at + j, sub), :] = out.astype(B16)
-        sums[first : first + 8, :] += eight_rows(out)
-        sums[first + 8 : first + 16, :] += eight_rows(by_n)
-        sums[first + 16 : first + 24, :] += eight_rows(du)
+        sums[first : first + 8, :] += eight_rows(by_n)
+        sums[first + 8 : first + 16, :] += eight_rows(dn)
 
     each_sub(count, body)
 
@@ -109,22 +108,24 @@
 def step_kernel(dims, *refs):
     rows, lat, act_width, in_width, hid, heads, bins, tasks, emb, steps = dims
     side_width = in_width - lat
-    block = in_width + hid + LANES + VECS
-    block0 = in_width + hid + lat + VECS
-    at_mid = in_width
-    at_out = in_width + hid
+    at_mid = in_width + VECS
+    at_out = at_mid + hid
+    block = at_out + padded(bins)
+    block0 = at_out + lat
     both = 2 * rows
+    ones_at = in_width // LANES * LANES
+    pieces = ((0, at_mid), (at_mid, at_out), (at_out, block0))
     (
         lat_in, acts, task, valid, bin_at, part_of, amask, table, cot_in, w_in, w_mid, w_dyn, w_q,
         b_in, g_in, s_in, b_mid, g_mid, s_mid, b_dyn, g_dyn, s_dyn, b_q,
         lat_out, grad_out, recv_q, recv_0, small_out,
         x, m, wi, wm, wq, wq_raw, wi0, wm0, wd, vec, bq, diag,
-        ig, act1, act2, spg, fpg, qg, n1, d1, n2, d2, q_scales, pre,
+        lines, acting, vec_lines, ig, act1, act2, spg, fpg, qg, n1, d1, n2, d2, q_scales, pre,
         act1_0, act2_0, spg_0, fpg_0, n1_0, d1_0, n2_0, d2_0, scales,
         dyn_n, new_lat, lat_low, cot, arrived, pair_grad, pair_send,
-        gb, half_q, half_0, sums, q_sums, dyn_sums, stat, small, small_recv, table_recv,
+        gb, half_q, half_0, sums, q_sums, dyn_sums, stat, small, small_mate, small_chips, small_half, small_steps, small_done,
         w_sem, in_sem, out_sem, lat_s, lat_r, px_s, px_r, side_s, side_r, pg_s, pg_r, gr_s, gr_r,
-        half_s, half_r, own_s, rb_s, rb_r, sm_s, sm_r, tb_s, tb_r, up_s, up_r, dn_s, dn_r, up_ok, dn_ok,
+        half_s, half_r, own_s, rb_s, rb_r, sm_s, sm_r, ch_s, ch_r, tb_s, tb_r, up_s, up_r, dn_s, dn_r, up_ok, dn_ok,
     ) = refs
     section = lax.axis_index("section")
     d = lax.axis_index("dp")
@@ -153,7 +154,7 @@
         return pl.multiple_of(i * CHUNK, CHUNK)
 
     loads = [
-        pltpu.make_async_copy(w_in.at[0], wi0, w_sem.at[0]),
+        pltpu.make_async_copy(w_in.at[0], wi0.at[0:in_width], w_sem.at[0]),
         pltpu.make_async_copy(w_mid.at[0], wm0, w_sem.at[1]),
         pltpu.make_async_copy(w_dyn, wd, w_sem.at[2]),
     ]
@@ -162,7 +163,7 @@
         slot = lax.rem(job, 2)
         h = first_head + job
         return [
-            pltpu.make_async_copy(w_in.at[h], wi.at[slot], w_sem.at[3 + 3 * slot]),
+            pltpu.make_async_copy(w_in.at[h], wi.at[slot, 0:in_width], w_sem.at[3 + 3 * slot]),
             pltpu.make_async_copy(w_mid.at[h], wm.at[slot], w_sem.at[4 + 3 * slot]),
             pltpu.make_async_copy(w_q.at[h - 1], wq_raw.at[slot], w_sem.at[5 + 3 * slot]),
         ]
@@ -172,17 +173,6 @@
     def load_lat(i):
         here = pl.ds(chunk_at(i), CHUNK)
         return pltpu.make_async_copy(lat_in.at[here], x.at[here, 0:lat], in_sem.at[i])
-
-    loads[0].start()
-
-    @pl.when(section == 0)
-    def _():
-        for i in range(chunks):
-            load_lat(i).start()
-
-    for copy in loads[1:] + job_loads(jnp.int32(0)) + job_loads(jnp.int32(1)):
-        copy.start()
-    load_cot.start()
 
     barrier = pltpu.get_barrier_semaphore()
     for other in range(1, PEERS):
@@ -192,49 +182,86 @@
         to = lax.rem(section + other, steps)
         pl.semaphore_signal(barrier, inc=1, device_id=(to, d), device_id_type=MESH)
 
-    lines = [task[...].astype(F32), valid[...].astype(F32), bin_at[...].astype(F32), part_of[...]]
-    lines.append(jnp.zeros((4, rows), F32))
-    m[0:rows, 0:8] = jnp.concatenate(lines, 0).T
+    loads[0].start()
+
+    @pl.when(section == 0)
+    def _():
+        for i in range(chunks):
+            load_lat(i).start()
+
+    for copy in loads[1:] + job_loads(jnp.int32(0)) + job_loads(jnp.int32(1)):
+        copy.start()
+    load_cot.start()
+
+    head_lines = [task[...].astype(F32), valid[...].astype(F32), bin_at[...].astype(F32), part_of[...]]
+    lines[0] = jnp.concatenate(head_lines + [jnp.zeros((4, rows), F32)], 0)
+    acting[0] = acts[...]
 
     def one_hot(lo, count):
         task_lane = lax.broadcasted_iota(jnp.int32, (count, tasks), 1).astype(F32)
         return (m[lo : lo + count, 0:1] == task_lane).astype(F32).astype(B16)
 
-    hot = one_hot(0, rows)
-    mask = dot(amask[...].astype(F32).astype(B16), hot, NT)
-    acting = (acts[...].astype(F32) * mask).T
-    side = jnp.concatenate([acting.astype(B16), dot(hot, table[...]).astype(B16)], 1)
-    x[0:rows, lat:in_width] = side
+    def prepare(which):
+        lo = which * rows
+        m[lo : lo + rows, 0:8] = lines[which].T
+        hot = one_hot(lo, rows)
+        mask = dot(amask[...].astype(F32).astype(B16), hot, NT)
+        used = (acting[which].astype(F32) * mask).T
+        x[lo : lo + rows, lat:in_width] = jnp.concatenate(
+            [used.astype(B16), dot(hot, table[...]).astype(B16)], 1
+        )
+
+    lane = lax.broadcasted_iota(jnp.int32, (both, LANES), 1)
+    x[:, ones_at : ones_at + LANES] = (lane == in_width - ones_at).astype(F32).astype(B16)
+    prepare(0)
     for t, source in enumerate((b_in, g_in, s_in, b_mid, g_mid, s_mid)):
         vec[t, 0 : heads + 1, :] = source[...].astype(F32)
-    bq[...] = jnp.full(bq.shape, -1e30, F32)
-    bq[0:heads, 0:bins] = b_q[...].astype(F32)
-    wq[...] = jnp.zeros(wq.shape, B16)
     shift = GROUP.bit_length() - 1
     diag[...] = (
         lax.shift_right_logical(lax.broadcasted_iota(jnp.int32, (lat, lat), 0), shift)
         == lax.shift_right_logical(lax.broadcasted_iota(jnp.int32, (lat, lat), 1), shift)
     ).astype(F32).astype(B16)
-    sums[...] = jnp.zeros(sums.shape, F32)
-    ig[...] = jnp.zeros(ig.shape, F32)
-    q_sums[...] = jnp.zeros(q_sums.shape, F32)
-    dyn_sums[...] = jnp.zeros(dyn_sums.shape, F32)
+
+    def bias_rows(h):
+        line = lax.broadcasted_iota(jnp.int32, (VECS, hid), 0)
+        return jnp.where(line == 0, vec[0, pl.ds(h, 1), :], 0.0).astype(B16)
+
+    wi0[in_width:at_mid, :] = bias_rows(0)
     stat[...] = jnp.zeros(stat.shape, F32)
-    small[...] = jnp.zeros(small.shape, F32)
+
+    def clear():
+        bq[...] = jnp.full(bq.shape, -1e30, F32)
+        bq[0:heads, 0:bins] = b_q[...].astype(F32)
+        wq[...] = jnp.zeros(wq.shape, B16)
+        sums[...] = jnp.zeros(sums.shape, F32)
+        ig[...] = jnp.zeros(ig.shape, F32)
+        q_sums[...] = jnp.zeros(q_sums.shape, F32)
+        dyn_sums[...] = jnp.zeros(dyn_sums.shape, F32)
+        small[...] = jnp.zeros(small.shape, F32)
+
+    pl.semaphore_wait(barrier, PEERS - 1 + steps - 1)
+
+    side_copies = [
+        remote(lines.at[0], lines.at[1], side_s.at[0], side_r.at[0], (section, pair)),
+        remote(acting.at[0], acting.at[1], side_s.at[1], side_r.at[1], (section, pair)),
+    ]
+    for copy in side_copies:
+        copy.start()
+
+    def settle():
+        clear()
+        for copy in side_copies:
+            copy.wait_recv()
+        prepare(1)
 
     @pl.when(section == last)
     def _():
         arrived[...] = jnp.zeros(arrived.shape, B16)
 
-    pl.semaphore_wait(barrier, PEERS - 1 + steps - 1)
-
-    side_copy = remote(
-        x.at[0:rows, lat : lat + 2 * LANES], x.at[rows:both, lat : lat + 2 * LANES],
-        side_s.at[0], side_r.at[0], (section, pair),
-    )
-    meta_copy = remote(m.at[0:rows], m.at[rows:both], side_s.at[1], side_r.at[1], (section, pair))
-    side_copy.start()
-    meta_copy.start()
+    @pl.when(section > 0)
+    def _():
+        settle()
+
     for copy in loads:
         copy.wait()
 
@@ -271,9 +298,9 @@
             load_lat(i).wait()
 
         pair_copy(i).start()
-        pre[0:CHUNK, :] = dot(x[here, 0:in_width], wi0[...])
+        pre[0:CHUNK, :] = dot(x[here, 0:at_mid], wi0[...])
         layer_forward(
-            pre, CHUNK, vec[0, 0:1, :], vec[1, 0:1, :], vec[2, 0:1, :], act1_0, at, n1_0, d1_0, scales, 0, at
+            pre, CHUNK, None, vec[1, 0:1, :], vec[2, 0:1, :], act1_0, at, n1_0, d1_0, scales, 0, at
         )
         pre[0:CHUNK, :] = dot(act1_0[here, :], wm0[...])
         layer_forward(
@@ -302,6 +329,10 @@
 
     lax.fori_loop(0, chunks, forward_chunk, 0)
 
+    @pl.when(section == 0)
+    def _():
+        settle()
+
     def pg_copy(i):
         here = pl.ds(chunk_at(i), CHUNK)
         return remote(
@@ -312,9 +343,9 @@
         here = pl.ds(at, QROWS)
         h = first_head + job
         slot = lax.rem(job, 2)
-        pre[...] = dot(x[here, 0:in_width], wi[slot])
+        pre[...] = dot(x[here, 0:at_mid], wi[slot])
         layer_forward(
-            pre, QROWS, vec_of(0, h), vec_of(1, h), vec_of(2, h), act1, at, n1, d1, q_scales, 0, 0
+            pre, QROWS, None, vec_of(1, h), vec_of(2, h), act1, at, n1, d1, q_scales, 0, 0
         )
         pre[...] = dot(act1[here, :], wm[slot])
         layer_forward(
@@ -331,9 +362,9 @@
         qg[here, :] = grad
         q_sums[job] += eight_rows(grad.astype(F32))
         pre[...] = dot(grad, wq[slot])
-        layer_backward(pre, QROWS, vec_of(4, h), n2, d2, q_scales, 1, 0, spg, at, sums.at[0], 24)
+        layer_backward(pre, QROWS, n2, d2, q_scales, 1, 0, spg, at, sums.at[0], 16)
         pre[...] = dot(spg[here, :], wm[slot], NT)
-        layer_backward(pre, QROWS, vec_of(1, h), n1, d1, q_scales, 0, 0, fpg, at, sums.at[0], 0)
+        layer_backward(pre, QROWS, n1, d1, q_scales, 0, 0, fpg, at, sums.at[0], 0)
         for lo, hi in tiles(in_width):
             ig[here, lo:hi] += dot(fpg[here, :], wi[slot, lo:hi, :], NT)
 
@@ -345,6 +376,7 @@
             copy.wait()
         slot = lax.rem(job, 2)
         wq[slot, 0:bins, :] = wq_raw[slot]
+        wi[slot, in_width:at_mid, :] = bias_rows(first_head + job)
         sums[0] = jnp.zeros(sums.shape[1:], F32)
 
         def body(i, carry):
@@ -353,9 +385,6 @@
 
             @pl.when((job == 0) & (which == own_chunks))
             def _():
-                side_copy.wait_recv()
-                meta_copy.wait_recv()
-
                 def pair_here(j, carry):
                     pair_copy(j).wait_recv()
                     return carry
@@ -406,27 +435,74 @@
             span = slice(part * step, size if part == 3 else (part + 1) * step)
             dst[span, :] = (dst[span, :].astype(F32) + src[span, :].astype(F32)).astype(B16)
 
+    def at_chip(z):
+        return (section, base + 2 * z + core)
+
+    def stripe(z):
+        return pl.ds(pl.multiple_of(z * LANES, LANES), LANES)
+
+    def up_piece(z, p):
+        size = pieces[p][1] - pieces[p][0]
+        return (act1.at[0:size, stripe(z)], act1.at[0:size, stripe(CHIPS + z)], act2.at[0:size, stripe(z)])[p]
+
+    def down_piece(z, p):
+        size = pieces[p][1] - pieces[p][0]
+        return (spg.at[0:size, stripe(z)], spg.at[0:size, stripe(CHIPS + z)], act2.at[0:size, stripe(CHIPS + z)])[p]
+
+    def up_copy(z, p):
+        return remote(
+            half_0.at[z, pieces[p][0] : pieces[p][1]], up_piece(z, p), up_s.at[z, p], up_r.at[z, p],
+            at_chip(jnp.minimum(chip + 1, CHIPS - 1)),
+        )
+
+    def down_copy(z, p):
+        return remote(
+            half_0.at[z, pieces[p][0] : pieces[p][1]], down_piece(z, p), dn_s.at[z, p], dn_r.at[z, p],
+            at_chip(jnp.maximum(chip - 1, 0)),
+        )
+
+    def add_piece(piece, z, p):
+        lo, hi = pieces[p]
+        half_0[z, lo:hi, :] = (half_0[z, lo:hi, :].astype(F32) + piece(z, p)[...].astype(F32)).astype(B16)
+
     def weight_grads(job, q):
         if q:
             count, a1, a2, sp, fp, own_sums = both, act1, act2, spg, fpg, 0
         else:
             count, a1, a2, sp, fp, own_sums = rows, act1_0, act2_0, spg_0, fpg_0, 1
         size = block if q else block0
+        h = first_head + job if q else 0
+        line_at = lax.broadcasted_iota(jnp.int32, (VECS, hid), 0)
+        vectors = jnp.zeros((VECS, hid), F32)
+        for t, (first, gain) in enumerate(((0, 1), (8, 1), (None, None), (16, 4), (24, 4))):
+            if gain is not None:
+                line = jnp.sum(sums[own_sums, first : first + 8, :], 0, keepdims=True) / vec_of(gain, h)
+                vectors = jnp.where(line_at == t + 1, line, vectors)
+        vec_lines[...] = vectors
+        row_at = lax.broadcasted_iota(jnp.int32, (VECS, 2 * LANES), 0)
 
         def order(i):
-            return jnp.where(lower, CHIPS - 1 - i, i)
+            far_first = jnp.where(lower, CHIPS - 1 - i, i)
+            pair_first = lax.rem(jnp.where(lower, CHIPS - i, i + CHIPS - 1), CHIPS)
+            return jnp.where(edge, far_first, pair_first)
 
         def make(z):
             cols = pl.ds(pl.multiple_of(z * 2 * LANES, 2 * LANES), 2 * LANES)
-            for left, right, first, size_of in ((x, fp, 0, in_width), (a1, sp, at_mid, hid)):
+            for left, right, first, size_of in ((x, fp, 0, at_mid), (a1, sp, at_mid, hid)):
                 for lo, hi in tiles(size_of):
                     grad = dot(left[0:count, lo:hi], right[0:count, cols], TN)
+                    if left is x and hi == at_mid:
+                        plain = grad[0 : in_width - lo]
+                        bias_mid = dot(x[0:count, ones_at : ones_at + LANES], sp[0:count, cols], TN)
+                        bias_mid = bias_mid[in_width - ones_at : in_width - ones_at + 1]
+                        lines_here = grad[in_width - lo :] + vec_lines[:, cols]
+                        grad = jnp.concatenate([plain, jnp.where(row_at == 3, bias_mid, lines_here)], 0)
                     for p in range(2):
                         gb[p, z, first + lo : first + hi, :] = grad[:, p * LANES : (p + 1) * LANES].astype(B16)
             if q:
                 g_out = dot(qg[0:count, :], a2[0:count, cols], TN)
                 for p in range(2):
-                    gb[p, z, at_out : at_out + LANES, :] = g_out[:, p * LANES : (p + 1) * LANES].astype(B16)
+                    gb[p, z, at_out:block, :] = g_out[0 : block - at_out, p * LANES : (p + 1) * LANES].astype(B16)
             else:
                 g_out = dot(a2[0:count, cols], arrived[0:count, :], TN)
                 for p in range(2):
@@ -434,11 +510,6 @@
                         gb[p, z, at_out + t * LANES : at_out + (t + 1) * LANES, :] = g_out[
                             p * LANES : (p + 1) * LANES, t * LANES : (t + 1) * LANES
                         ].astype(B16)
-            lines = [jnp.sum(sums[own_sums, 8 * t : 8 * t + 8, cols], 0, keepdims=True) for t in range(6)]
-            lines.append(jnp.zeros((VECS - 6, 2 * LANES), F32))
-            vectors = jnp.concatenate(lines, 0).astype(B16)
-            for p in range(2):
-                gb[p, z, size - VECS : size, :] = vectors[:, p * LANES : (p + 1) * LANES]
             half_copy(job, z, q).start()
 
         def finish(z):
@@ -456,11 +527,26 @@
             else:
                 add_rows(half_0.at[z], gb.at[core, z], size)
 
+                @pl.when((chip == 0) & (z != chip))
+                def _():
+                    for p in range(3):
+                        up_copy(z, p).start()
+
+                @pl.when((chip == CHIPS - 1) & (z != chip))
+                def _():
+                    for p in range(3):
+                        down_copy(z, p).start()
+
         def body(i, carry):
             @pl.when(i < CHIPS)
             def _():
                 make(order(i))
 
+            if not q:
+                @pl.when(i == 1)
+                def _():
+                    small_over_chips()
+
             @pl.when(i > 0)
             def _():
                 finish(order(i - 1))
@@ -474,17 +560,6 @@
             return carry
 
         lax.fori_loop(0, CHIPS, sent, 0)
-
-    def job_body(job, carry):
-        q_job(job)
-
-        @pl.when(job < jobs - 1)
-        def _():
-            weight_grads(job, True)
-
-        return carry
-
-    lax.fori_loop(0, jobs, job_body, 0)
 
     def back_copy(i):
         here = pl.ds(chunk_at(i), CHUNK)
@@ -526,10 +601,10 @@
         dyn_sums[8:16, :] += eight_rows(by_n)
         dyn_sums[16:24, :] += eight_rows(norm_grad)
         pre[0:CHUNK, :] = dot(low, wd[...], NT)
-        layer_backward(pre, CHUNK, vec[4, 0:1, :], n2_0, d2_0, scales, 1, at, spg_0, at, sums.at[1], 24)
+        layer_backward(pre, CHUNK, n2_0, d2_0, scales, 1, at, spg_0, at, sums.at[1], 16)
         pre[0:CHUNK, :] = dot(spg_0[here, :], wm0[...], NT)
-        layer_backward(pre, CHUNK, vec[1, 0:1, :], n1_0, d1_0, scales, 0, at, fpg_0, at, sums.at[1], 0)
-        back_in = dot(fpg_0[here, :], wi0[...], NT)
+        layer_backward(pre, CHUNK, n1_0, d1_0, scales, 0, at, fpg_0, at, sums.at[1], 0)
+        back_in = dot(fpg_0[here, :], wi0[0:in_width, :], NT)
         pg_copy(i).wait_recv()
         total = back_in[:, 0:lat] + ig[here, 0:lat] + pair_grad[here, :].astype(F32)
         lat_low[here, :] = total.astype(B16)
@@ -544,13 +619,72 @@
         ig[here, lat:in_width] += back_in[:, lat:in_width]
         return carry
 
-    def small_copy(other):
-        to = base + lax.rem(place + other, PEERS)
-        return remote(small, small_recv.at[place], sm_s.at[other], sm_r.at[place], (section, to))
-
-    def small_arrival(other):
-        source = lax.rem(place + other, PEERS)
-        return remote(small, small_recv.at[source], sm_s.at[other], sm_r.at[source], (section, base + source))
+    half_rows = small.shape[0] // 2
+    my_rows = pl.ds(pl.multiple_of(core * half_rows, half_rows), half_rows)
+
+    def to_mate(src, dst, k):
+        return remote(src, dst, sm_s.at[k], sm_r.at[k], (section, mate))
+
+    def small_to_mate():
+        return to_mate(small, small_mate, 0)
+
+    def small_to_chip(other):
+        to = lax.rem(chip + other, CHIPS)
+        return remote(
+            small.at[my_rows], small_chips.at[chip], ch_s.at[other], ch_r.at[chip], (section, base + 2 * to + core)
+        )
+
+    def small_from_chip(other):
+        to = lax.rem(chip + other, CHIPS)
+        return remote(
+            small.at[my_rows], small_chips.at[to], ch_s.at[other], ch_r.at[to], (section, base + 2 * to + core)
+        )
+
+    def small_to_section(other):
+        to = lax.rem(section + other, steps)
+        return remote(small_half, small_steps.at[section], tb_s.at[other], tb_r.at[section], (to, d))
+
+    def small_from_section(other):
+        source = lax.rem(section + other, steps)
+        return remote(small_half, small_steps.at[source], tb_s.at[other], tb_r.at[source], (source, d))
+
+    def small_back():
+        return to_mate(small_done.at[my_rows], small_done.at[my_rows], 1)
+
+    def small_over_chips():
+        small_to_mate().wait_recv()
+        small_to_mate().wait_send()
+        small[...] += small_mate[...]
+        small_chips[chip] = small[my_rows, :]
+        for other in range(1, CHIPS):
+            small_to_chip(other).start()
+
+    def small_over_sections():
+        for other in range(1, CHIPS):
+            small_from_chip(other).wait_recv()
+        total = small_chips[0]
+        for source in range(1, CHIPS):
+            total = total + small_chips[source]
+        small_half[...] = total
+        small_steps[section] = total
+        for other in range(1, steps):
+            small_to_section(other).start()
+
+    def small_last():
+        for other in range(1, steps):
+            small_from_section(other).wait_recv()
+        whole = small_steps[0]
+        for source in range(1, steps):
+            whole = whole + small_steps[source]
+        row = lax.broadcasted_iota(jnp.int32, whole.shape, 0) + core * half_rows
+        small_done[my_rows, :] = jnp.where(row < tasks, whole, small_half[...])
+        small_back().start()
+        for other in range(1, CHIPS):
+            small_to_chip(other).wait_send()
+        for other in range(1, steps):
+            small_to_section(other).wait_send()
+        small_back().wait_recv()
+        small_back().wait_send()
 
     def send_small():
         table_part = jnp.zeros((tasks, side_width), F32)
@@ -577,36 +711,27 @@
         small[row : row + 1, :] = jnp.where(
             lane == 0, count, jnp.where(lane == 1, lat_square, jnp.where(lane == 2, grad_square, 0.0))
         )
-        small_recv[place] = small[...]
-        for other in range(1, PEERS):
-            small_copy(other).start()
-
-    load_cot.wait()
-    lax.fori_loop(0, chunks, lat_sent, 0)
-
-    def late(turn, carry):
-        @pl.when((turn == 0) == (section == last))
-        def _():
+        small_to_mate().start()
+
+    def turns(turn, carry):
+        @pl.when(turn < jobs)
+        def _():
+            q_job(turn)
+
+        @pl.when(turn == jobs)
+        def _():
+            load_cot.wait()
+            lax.fori_loop(0, chunks, lat_sent, 0)
             lax.fori_loop(0, chunks, backward_chunk, 0)
             send_small()
 
-        @pl.when((turn == 0) == (section < last))
-        def _():
-            weight_grads(jobs - 1, True)
+        @pl.when((turn < jobs - 1) | ((turn == jobs - 1) & (section < last)) | ((turn == jobs) & (section == last)))
+        def _():
+            weight_grads(jnp.minimum(turn, jobs - 1), True)
 
         return carry
 
-    lax.fori_loop(0, 2, late, 0)
-    weight_grads(jnp.int32(3), False)
-
-    def at_chip(z):
-        return (section, base + 2 * z + core)
-
-    def up_copy(t):
-        return remote(half_0.at[t], gb.at[0, t], up_s.at[t], up_r.at[t], at_chip(jnp.minimum(chip + 1, CHIPS - 1)))
-
-    def down_copy(t):
-        return remote(half_0.at[t], gb.at[1, t], dn_s.at[t], dn_r.at[t], at_chip(jnp.maximum(chip - 1, 0)))
+    lax.fori_loop(0, jobs + 1, turns, 0)
 
     @pl.when(chip > 0)
     def _():
@@ -618,62 +743,47 @@
             dn_ok, inc=1, device_id=at_chip(jnp.minimum(chip + 1, CHIPS - 1)), device_id_type=MESH
         )
 
+    @pl.when(chip < CHIPS - 1)
+    def _():
+        pl.semaphore_wait(up_ok, 1)
+
+    @pl.when(chip > 0)
+    def _():
+        pl.semaphore_wait(dn_ok, 1)
+
+    weight_grads(jnp.int32(3), False)
+
     def hops(turn, carry):
-        @pl.when(((turn == 0) == lower) & (chip < CHIPS - 1))
-        def _():
-            pl.semaphore_wait(up_ok, 1)
-            for t in range(CHIPS - 1, 0, -1):
+        @pl.when(((turn == 0) == lower) & ~edge)
+        def _():
+            for t in range(CHIPS - 1, 1, -1):
                 @pl.when(t > chip)
                 def _():
-                    @pl.when(chip > 0)
-                    def _():
-                        up_copy(t).wait_recv()
-                        add_rows(half_0.at[t], gb.at[0, t], block0)
-
-                    up_copy(t).start()
-
-        @pl.when(((turn == 0) != lower) & (chip > 0))
-        def _():
-            pl.semaphore_wait(dn_ok, 1)
-            for t in range(CHIPS - 1):
+                    for p in range(3):
+                        up_copy(t, p).wait_recv()
+                        add_piece(up_piece, t, p)
+                        up_copy(t, p).start()
+
+        @pl.when(((turn == 0) != lower) & ~edge)
+        def _():
+            for t in range(CHIPS - 2):
                 @pl.when(t < chip)
                 def _():
-                    @pl.when(chip < CHIPS - 1)
-                    def _():
-                        down_copy(t).wait_recv()
-                        add_rows(half_0.at[t], gb.at[1, t], block0)
-
-                    down_copy(t).start()
+                    for p in range(3):
+                        down_copy(t, p).wait_recv()
+                        add_piece(down_piece, t, p)
+                        down_copy(t, p).start()
+
+        @pl.when(turn == 0)
+        def _():
+            small_over_sections()
 
         return carry
 
     lax.fori_loop(0, 2, hops, 0)
 
-    for other in range(1, PEERS):
-        small_arrival(other).wait_recv()
-    total = small_recv[0]
-    for source in range(1, PEERS):
-        total = total + small_recv[source]
-    for other in range(1, PEERS):
-        small_copy(other).wait_send()
-    small[...] = total
-    table_recv[section] = small[0:tasks, :]
-
-    def table_copy(other):
-        to = lax.rem(section + other, steps)
-        return remote(
-            small.at[0:tasks], table_recv.at[section], tb_s.at[other], tb_r.at[section], (to, d)
-        )
-
-    def table_arrival(other):
-        source = lax.rem(section + other, steps)
-        return remote(small.at[0:tasks], table_recv.at[source], tb_s.at[other], tb_r.at[source], (source, d))
-
-    for other in range(1, steps):
-        table_copy(other).start()
-
-    side_copy.wait_send()
-    meta_copy.wait_send()
+    for copy in side_copies:
+        copy.wait_send()
 
     def sends(i, carry):
         pair_copy(i).wait_send()
@@ -710,34 +820,31 @@
 
     @pl.when(chip > 0)
     def _():
-        up_copy(chip).wait_recv()
-        add_rows(half_0.at[chip], gb.at[0, chip], block0)
+        for p in range(3):
+            up_copy(chip, p).wait_recv()
+            add_piece(up_piece, chip, p)
 
     @pl.when(chip < CHIPS - 1)
     def _():
-        down_copy(chip).wait_recv()
-        add_rows(half_0.at[chip], gb.at[1, chip], block0)
+        for p in range(3):
+            down_copy(chip, p).wait_recv()
+            add_piece(down_piece, chip, p)
 
     keep_0 = pltpu.make_async_copy(half_0.at[chip], recv_0, own_s.at[3])
     keep_0.start()
     for t in range(CHIPS):
         @pl.when(t > chip)
         def _():
-            up_copy(t).wait_send()
+            for p in range(3):
+                up_copy(t, p).wait_send()
 
         @pl.when(t < chip)
         def _():
-            down_copy(t).wait_send()
-
-    for other in range(1, steps):
-        table_arrival(other).wait_recv()
-    for other in range(1, steps):
-        table_copy(other).wait_send()
-    whole = table_recv[0]
-    for source in range(1, steps):
-        whole = whole + table_recv[source]
-    small[0:tasks, :] = whole
-    done = pltpu.make_async_copy(small, small_out, out_sem.at[2 * chunks])
+            for p in range(3):
+                down_copy(t, p).wait_send()
+
+    small_last()
+    done = pltpu.make_async_copy(small_done, small_out, out_sem.at[2 * chunks])
     done.start()
     done.wait()
     keep_0.wait()
@@ -745,36 +852,50 @@
 
 def finish_kernel(dims, *refs):
     lat, in_width, hid, heads, bins, tasks, emb = dims
-    block = in_width + hid + LANES + VECS
-    block0 = in_width + hid + lat + VECS
-    at_out = in_width + hid
-    recv_q, recv_0, small, lat_in, grad_in = refs[:5]
+    at_mid = in_width + VECS
+    at_out = at_mid + hid
+    recv_q, recv_0, small_in, lat_in, grad_in = refs[:5]
     lat_out, grad_out, w_in, w_mid, w_dyn, w_q, b_dyn, g_dyn, s_dyn, b_q, table, rms = refs[5:17]
     vecs = refs[17:23]
-    sem = refs[23]
+    part_q, part_0, small, sum_in, sum_mid, lat_held, grad_held, in_sem, out_sem = refs[23:]
+    loads = [pltpu.make_async_copy(recv_0, part_0, in_sem.at[0])]
+    loads += [pltpu.make_async_copy(recv_q.at[h], part_q.at[h], in_sem.at[1 + h]) for h in range(heads)]
+    load_small = pltpu.make_async_copy(small_in, small, in_sem.at[1 + heads])
+    through = [
+        pltpu.make_async_copy(lat_in, lat_held, in_sem.at[2 + heads]),
+        pltpu.make_async_copy(grad_in, grad_held, in_sem.at[3 + heads]),
+    ]
     copies = [
-        pltpu.make_async_copy(lat_in, lat_out, sem.at[0]),
-        pltpu.make_async_copy(grad_in, grad_out, sem.at[1]),
+        pltpu.make_async_copy(lat_held, lat_out, out_sem.at[0]),
+        pltpu.make_async_copy(grad_held, grad_out, out_sem.at[1]),
     ]
-    for copy in copies:
+    for copy in through + loads + [load_small]:
         copy.start()
 
     def total(h, lo, hi):
         if h == 0:
-            return recv_0[lo:hi, :].astype(F32)
-        return recv_q[h - 1, 0, lo:hi, :].astype(F32) + recv_q[h - 1, 1, lo:hi, :].astype(F32)
-
+            return part_0[lo:hi, :].astype(F32)
+        return part_q[h - 1, 0, lo:hi, :].astype(F32) + part_q[h - 1, 1, lo:hi, :].astype(F32)
+
+    for arriving, leaving in zip(through, copies):
+        arriving.wait()
+        leaving.start()
     for h in range(heads + 1):
-        w_in[h] = total(h, 0, in_width)
-        w_mid[h] = total(h, in_width, at_out)
-        size = block if h else block0
-        lines = total(h, size - VECS, size)
+        loads[h].wait()
+        sum_in[h] = total(h, 0, in_width)
+        sum_mid[h] = total(h, at_mid, at_out)
+        copies.append(pltpu.make_async_copy(sum_in.at[h], w_in.at[h], out_sem.at[2 + 2 * h]))
+        copies.append(pltpu.make_async_copy(sum_mid.at[h], w_mid.at[h], out_sem.at[3 + 2 * h]))
+        for copy in copies[-2:]:
+            copy.start()
+        lines = total(h, in_width, at_mid)
         for t in range(6):
             vecs[t][h] = lines[t : t + 1, :]
         if h:
-            w_q[h - 1] = total(h, at_out, at_out + LANES)[0:bins, :]
+            w_q[h - 1] = total(h, at_out, at_out + padded(bins))[0:bins, :].reshape(bins, 1, LANES)
     for t in range(lat // LANES):
         w_dyn[:, t * LANES : (t + 1) * LANES] = total(0, at_out + t * LANES, at_out + (t + 1) * LANES)
+    load_small.wait()
     table[...] = small[0:tasks, 0:emb]
     for t, out in enumerate((b_dyn, g_dyn, s_dyn)):
         for part in range(lat // LANES):
@@ -805,13 +926,14 @@
     heads = w_q_out.shape[1]
     bin_count = w_q_out.shape[-1]
     tasks, emb = table.shape
-    block = in_width + hid + LANES + VECS
-    block0 = in_width + hid + lat + VECS
+    block = in_width + VECS + hid + padded(bin_count)
+    block0 = in_width + VECS + hid + lat
     chunks = rows // CHUNK
-    small_rows = tasks + 24
+    small_rows = padded(tasks + 3 * (lat // LANES) + heads + 1)
     dims = (rows, lat, act_width, in_width, hid, heads, bin_count, tasks, emb, steps)
     anywhere = pl.BlockSpec(memory_space=pl.ANY)
     vmem = pl.BlockSpec(memory_space=pltpu.VMEM)
+    hbm = pl.BlockSpec(memory_space=pltpu.HBM)
     dma = pltpu.SemaphoreType.DMA
     both = 2 * rows
     wide = pltpu.VMEM((rows, hid), B16)
@@ -833,16 +955,19 @@
         scratch_shapes=[
             pltpu.VMEM((both, 6 * LANES), B16),
             pltpu.VMEM((both, LANES), F32),
-            pltpu.VMEM((2, in_width, hid), B16),
+            pltpu.VMEM((2, in_width + VECS, hid), B16),
             pltpu.VMEM((2, hid, hid), B16),
             pltpu.VMEM((2, LANES, hid), B16),
             pltpu.VMEM((2, bin_count, hid), B16),
-            pltpu.VMEM((in_width, hid), B16),
+            pltpu.VMEM((in_width + VECS, hid), B16),
             pltpu.VMEM((hid, hid), B16),
             pltpu.VMEM((hid, lat), B16),
             pltpu.VMEM((6, 8, hid), F32),
             pltpu.VMEM((8, LANES), F32),
             pltpu.VMEM((lat, lat), B16),
+            pltpu.VMEM((2, 8, rows), F32),
+            pltpu.VMEM((2, act_width, rows), B16),
+            pltpu.VMEM((VECS, hid), F32),
             pltpu.VMEM((both, in_width), F32),
             q_wide, q_wide, q_wide, q_wide,
             pltpu.VMEM((both, LANES), B16),
@@ -856,19 +981,22 @@
             pltpu.VMEM((2, CHIPS, block0, LANES), B16),
             pltpu.VMEM((3, CHIPS, block, LANES), B16),
             pltpu.VMEM((CHIPS, block0, LANES), B16),
-            pltpu.VMEM((2, 48, hid), F32),
+            pltpu.VMEM((2, 32, hid), F32),
             pltpu.VMEM((3, 8, LANES), F32),
             pltpu.VMEM((24, lat), F32),
             pltpu.VMEM((16, lat), F32),
             pltpu.VMEM((small_rows, LANES), F32),
-            pltpu.VMEM((PEERS, small_rows, LANES), F32),
-            pltpu.VMEM((steps, tasks, LANES), F32),
+            pltpu.VMEM((small_rows, LANES), F32),
+            pltpu.VMEM((CHIPS, small_rows // 2, LANES), F32),
+            pltpu.VMEM((small_rows // 2, LANES), F32),
+            pltpu.VMEM((steps, small_rows // 2, LANES), F32),
+            pltpu.VMEM((small_rows, LANES), F32),
             dma((10,)), dma((chunks,)), dma((2 * chunks + 1,)),
             dma((chunks,)), dma((chunks,)), dma((chunks,)), dma((chunks,)),
             dma((2,)), dma((2,)), dma((chunks,)), dma((chunks,)), dma((chunks,)), dma((chunks,)),
             dma((4, CHIPS)), dma((4, CHIPS)), dma((4,)), dma((3, CHIPS)), dma((heads, 2)),
-            dma((PEERS,)), dma((PEERS,)), dma((steps,)), dma((steps,)),
-            dma((CHIPS,)), dma((CHIPS,)), dma((CHIPS,)), dma((CHIPS,)),
+            dma((2,)), dma((2,)), dma((CHIPS,)), dma((CHIPS,)), dma((steps,)), dma((steps,)),
+            dma((CHIPS, 3)), dma((CHIPS, 3)), dma((CHIPS, 3)), dma((CHIPS, 3)),
             pltpu.SemaphoreType.REGULAR, pltpu.SemaphoreType.REGULAR,
         ],
         compiler_params=pltpu.CompilerParams(
@@ -898,16 +1026,26 @@
                 shape(heads + 1, in_width, LANES),
                 shape(heads + 1, hid, LANES),
                 shape(LANES, lat),
-                shape(heads, bin_count, LANES),
+                shape(heads, bin_count, 1, LANES),
                 shape(1, lat), shape(1, lat), shape(1, lat),
                 shape(heads, 1, bin_count),
                 shape(tasks, emb),
                 shape(1, 2),
             ] + [shape(heads + 1, 1, LANES)] * 6,
-            in_specs=[vmem] * 3 + [anywhere] * 2,
-            out_specs=[anywhere] * 2 + [vmem] * 16,
-            scratch_shapes=[dma((2,))],
-            compiler_params=pltpu.CompilerParams(vmem_limit_bytes=40 * 2**20),
+            in_specs=[hbm] * 5,
+            out_specs=[hbm] * 4 + [vmem] * 14,
+            scratch_shapes=[
+                pltpu.VMEM((heads, 2, block, LANES), B16),
+                pltpu.VMEM((block0, LANES), B16),
+                pltpu.VMEM((small_rows, LANES), F32),
+                pltpu.VMEM((heads + 1, in_width, LANES), F32),
+                pltpu.VMEM((heads + 1, hid, LANES), F32),
+                pltpu.VMEM((rows, lat), B16),
+                pltpu.VMEM((rows, lat), F32),
+                dma((heads + 4,)),
+                dma((2 * heads + 4,)),
+            ],
+            compiler_params=pltpu.CompilerParams(vmem_limit_bytes=60 * 2**20),
             name="finish",
         )(recv_q, recv_0, small, lat_out, grad_out)
     )
@@ -919,7 +1057,7 @@
         moves = [(q * PEERS + r, r * groups + q) for q in range(groups) for r in range(PEERS)]
         return lax.ppermute(piece, "dp", moves)
 
-    part_in, part_mid, part_q = owned(part_in, 2), owned(part_mid, 2), owned(part_q, 2)
+    part_in, part_mid, part_q = owned(part_in, 2), owned(part_mid, 2), owned(part_q, 3)
     part_dyn = owned(part_dyn, 0)
     vecs = [owned(v, 2).transpose(1, 0, 2) for v in vecs]
     return (
@@ -933,7 +1071,7 @@
         b_dyn,
         g_dyn,
         s_dyn,
-        part_q.transpose(0, 2, 1)[None],
+        part_q.transpose(2, 0, 3, 1),
         q_bias.transpose(1, 0, 2),
         grad_table,
         rms,

time: 218 us -> 212 us (0.972); the launches traced: 218 us -> 209 us
  local copies, waits for them, and re-layouts: 7.42 us -> 0 us
    unnamed x11 -> x0, local copies, waits for them, and re-layouts: 7.42 us -> none
    pallas_call x1, Pallas kernels: 206 us -> 202 us  [on_device(): pl.pallas_call(functools.partial(step_kernel, dims), out_shape=[jax.Shape...]
    pallas_call x1, Pallas kernels: 3.7 us -> 6.76 us  [on_device(): pl.pallas_call(functools.partial(finish_kernel, (lat, in_width, hid, head...]
where the time goes in v3:
time: 212 us; the launch traced here: 209 us
  Pallas kernels  208 us (98%)
    pallas_call x1, Pallas kernels, on_device(): pl.pallas_call(functools.partial(step_kernel, dims), out_shape=[jax.Shape...  202 us
    pallas_call x1, Pallas kernels, on_device(): pl.pallas_call(functools.partial(finish_kernel, (lat, in_width, hid, head...  6.76 us

profile of v3, /device:TPU:14, one launch (start us, length us, event | category | flops | bytes accessed | tf_op | source)
XLA Modules:
  0.0 209.3 jit_solution(9661227796566511025)
XLA Ops:
  0.7 201.7 %step.1 = (bf16[512,512]{1,0:T(8,128)(2,1)}, f32[512,512]{1,0:T(8,128)}, bf16[5,2,1824,128]{3,2,1,0:T(8,128)(2,1)}, bf16[2224,128]{1,0:T(8,128)(2,1)}, f32[112,128]{1,0:T(8,128)}) custom-call(bf16[512,512]{1,0:T(8,128)(2,1)} %refs_0_.1, bf16[64,512]{1,0:T(8,128)(2,1)} %bitcast.38, s32[1,512]{1,0:T(1,128)} %bitcast.46, s32[1,512]{1,0:T(1,128)} %bitcast.47, ...), custom_call_target="tpu_custom_call" | custom-call | tf_op jit(solution)/shard_map/step/pallas_call | solution.py:944
  202.4 6.8 %finish.1 = (bf16[512,512]{1,0:T(8,128)(2,1)}, f32[512,512]{1,0:T(8,128)}, f32[6,672,128]{2,1,0:T(8,128)}, f32[6,1024,128]{2,1,0:T(8,128)}, f32[128,512]{1,0:T(8...) custom-call(bf16[5,2,1824,128]{3,2,1,0:T(8,128)(2,1)} %get-tuple-ele, ...), custom_call_target="tpu_custom_call" | custom-call | tf_op jit(solution)/shard_map/finish/pallas_call | solution.py:1021

commit v4 on v3

--- a/solution.py
+++ b/solution.py
@@ -218,9 +218,15 @@
         vec[t, 0 : heads + 1, :] = source[...].astype(F32)
     shift = GROUP.bit_length() - 1
     diag[...] = (
-        lax.shift_right_logical(lax.broadcasted_iota(jnp.int32, (lat, lat), 0), shift)
-        == lax.shift_right_logical(lax.broadcasted_iota(jnp.int32, (lat, lat), 1), shift)
+        lax.shift_right_logical(lax.broadcasted_iota(jnp.int32, diag.shape, 0), shift)
+        == lax.shift_right_logical(lax.broadcasted_iota(jnp.int32, diag.shape, 1), shift)
     ).astype(F32).astype(B16)
+
+    def group_sums(values):
+        width = diag.shape[0]
+        return jnp.concatenate(
+            [split_dot(values[:, lo : lo + width], diag[...]) for lo in range(0, lat, width)], 1
+        )
 
     def bias_rows(h):
         line = lax.broadcasted_iota(jnp.int32, (VECS, hid), 0)
@@ -313,7 +319,7 @@
         dyn_n[here, :] = normal.astype(B16)
         scales[here, 2:3] = scale
         power = jnp.exp(normal * g_dyn[...].astype(F32) + s_dyn[...].astype(F32))
-        fresh = power * pltpu.reciprocal(split_dot(power, diag[...]), approx=True)
+        fresh = power * pltpu.reciprocal(group_sums(power), approx=True)
         new_lat[here, :] = fresh
         low = fresh.astype(B16)
         lat_low[here, :] = low
@@ -589,7 +595,7 @@
         out_grad = cot[here, :].astype(F32) + arrived[here, :].astype(F32)
         fresh = new_lat[here, :]
         normal = dyn_n[here, :].astype(F32)
-        norm_grad = fresh * (out_grad - split_dot(out_grad * fresh, diag[...]))
+        norm_grad = fresh * (out_grad - group_sums(out_grad * fresh))
         by_n = norm_grad * normal
         gain = g_dyn[...].astype(F32)
         dm = norm_grad * gain
@@ -782,6 +788,10 @@
 
     lax.fori_loop(0, 2, hops, 0)
 
+    small_last()
+    done = pltpu.make_async_copy(small_done, small_out, out_sem.at[2 * chunks])
+    done.start()
+
     for copy in side_copies:
         copy.wait_send()
 
@@ -843,9 +853,6 @@
             for p in range(3):
                 down_copy(t, p).wait_send()
 
-    small_last()
-    done = pltpu.make_async_copy(small_done, small_out, out_sem.at[2 * chunks])
-    done.start()
     done.wait()
     keep_0.wait()
 
@@ -869,7 +876,8 @@
         pltpu.make_async_copy(lat_held, lat_out, out_sem.at[0]),
         pltpu.make_async_copy(grad_held, grad_out, out_sem.at[1]),
     ]
-    for copy in through + loads + [load_small]:
+    order = list(range(1, heads + 1)) + [0]
+    for copy in [loads[h] for h in order] + through + [load_small]:
         copy.start()
 
     def total(h, lo, hi):
@@ -877,13 +885,10 @@
             return part_0[lo:hi, :].astype(F32)
         return part_q[h - 1, 0, lo:hi, :].astype(F32) + part_q[h - 1, 1, lo:hi, :].astype(F32)
 
-    for arriving, leaving in zip(through, copies):
-        arriving.wait()
-        leaving.start()
-    for h in range(heads + 1):
+    for h in order:
         loads[h].wait()
+        sum_mid[h] = total(h, at_mid, at_out)
         sum_in[h] = total(h, 0, in_width)
-        sum_mid[h] = total(h, at_mid, at_out)
         copies.append(pltpu.make_async_copy(sum_in.at[h], w_in.at[h], out_sem.at[2 + 2 * h]))
         copies.append(pltpu.make_async_copy(sum_mid.at[h], w_mid.at[h], out_sem.at[3 + 2 * h]))
         for copy in copies[-2:]:
@@ -893,6 +898,9 @@
             vecs[t][h] = lines[t : t + 1, :]
         if h:
             w_q[h - 1] = total(h, at_out, at_out + padded(bins))[0:bins, :].reshape(bins, 1, LANES)
+    for arriving, leaving in zip(through, copies):
+        arriving.wait()
+        leaving.start()
     for t in range(lat // LANES):
         w_dyn[:, t * LANES : (t + 1) * LANES] = total(0, at_out + t * LANES, at_out + (t + 1) * LANES)
     load_small.wait()
@@ -964,7 +972,7 @@
             pltpu.VMEM((hid, lat), B16),
             pltpu.VMEM((6, 8, hid), F32),
             pltpu.VMEM((8, LANES), F32),
-            pltpu.VMEM((lat, lat), B16),
+            pltpu.VMEM((2 * LANES, 2 * LANES), B16),
             pltpu.VMEM((2, 8, rows), F32),
             pltpu.VMEM((2, act_width, rows), B16),
             pltpu.VMEM((VECS, hid), F32),

time: 212 us -> 210 us (level)
  no operation moved by 1% of the time
where the time goes in v4:
time: 210 us; the launch traced here: 208 us
  Pallas kernels  207 us (99%)
    pallas_call x1, Pallas kernels, on_device(): pl.pallas_call(functools.partial(step_kernel, dims), out_shape=[jax.Shape...  200 us
    pallas_call x1, Pallas kernels, on_device(): pl.pallas_call(functools.partial(finish_kernel, (lat, in_width, hid, head...  6.91 us

profile of v4, /device:TPU:14, one launch (start us, length us, event | category | flops | bytes accessed | tf_op | source)
XLA Modules:
  0.0 207.9 jit_solution(6834310293984991502)
XLA Ops:
  0.7 200.1 %step.1 = (bf16[512,512]{1,0:T(8,128)(2,1)}, f32[512,512]{1,0:T(8,128)}, bf16[5,2,1824,128]{3,2,1,0:T(8,128)(2,1)}, bf16[2224,128]{1,0:T(8,128)(2,1)}, f32[112,128]{1,0:T(8,128)}) custom-call(bf16[512,512]{1,0:T(8,128)(2,1)} %refs_0_.1, bf16[64,512]{1,0:T(8,128)(2,1)} %bitcast.38, s32[1,512]{1,0:T(1,128)} %bitcast.46, s32[1,512]{1,0:T(1,128)} %bitcast.47, ...), custom_call_target="tpu_custom_call" | custom-call | tf_op jit(solution)/shard_map/step/pallas_call | solution.py:952
  200.8 6.9 %finish.1 = (bf16[512,512]{1,0:T(8,128)(2,1)}, f32[512,512]{1,0:T(8,128)}, f32[6,672,128]{2,1,0:T(8,128)}, f32[6,1024,128]{2,1,0:T(8,128)}, f32[128,512]{1,0:T(8...) custom-call(bf16[5,2,1824,128]{3,2,1,0:T(8,128)(2,1)} %get-tuple-ele, ...), custom_call_target="tpu_custom_call" | custom-call | tf_op jit(solution)/shard_map/finish/pallas_call | solution.py:1029

commit v5 on v4

--- a/solution.py
+++ b/solution.py
@@ -143,6 +143,8 @@
     before = jnp.maximum(section - 1, 0)
     chunks = rows // CHUNK
     jobs = jnp.where(edge, 2, 3)
+    held = (section == steps - 1) & edge
+    farthest = CHIPS - 1 - chip
     first_head = jnp.where(edge, 1, 3)
 
     def remote(src, dst, send, recv, to):
@@ -523,7 +525,7 @@
             if q:
                 add_rows(half_q.at[job, z], gb.at[core, z], size)
 
-                @pl.when(z != chip)
+                @pl.when((z != chip) & ~((job == jobs - 1) & held & (z == farthest)))
                 def _():
                     owner_copy(job, z).start()
 
@@ -612,6 +614,11 @@
         layer_backward(pre, CHUNK, n1_0, d1_0, scales, 0, at, fpg_0, at, sums.at[1], 0)
         back_in = dot(fpg_0[here, :], wi0[0:in_width, :], NT)
         pg_copy(i).wait_recv()
+
+        @pl.when((i == chunks - 1) & held)
+        def _():
+            owner_copy(jobs - 1, farthest).start()
+
         total = back_in[:, 0:lat] + ig[here, 0:lat] + pair_grad[here, :].astype(F32)
         lat_low[here, :] = total.astype(B16)
 
@@ -719,6 +726,8 @@
         )
         small_to_mate().start()
 
+    waits = (section == last) & ~edge
+
     def turns(turn, carry):
         @pl.when(turn < jobs)
         def _():
@@ -731,7 +740,7 @@
             lax.fori_loop(0, chunks, backward_chunk, 0)
             send_small()
 
-        @pl.when((turn < jobs - 1) | ((turn == jobs - 1) & (section < last)) | ((turn == jobs) & (section == last)))
+        @pl.when((turn < jobs - 1) | ((turn == jobs - 1) & ~waits) | ((turn == jobs) & waits))
         def _():
             weight_grads(jnp.minimum(turn, jobs - 1), True)
 

time: 210 us -> 203 us (0.967)
  the two profiles are of different devices: /device:TPU:14 before, /device:TPU:0 now
where the time goes in v5:
time: 203 us
  Pallas kernels  202 us (100%)
    pallas_call x1, Pallas kernels, on_device(): pl.pallas_call(functools.partial(step_kernel, dims), out_shape=[jax.Shape...  195 us
    pallas_call x1, Pallas kernels, on_device(): pl.pallas_call(functools.partial(finish_kernel, (lat, in_width, hid, head...  6.91 us

profile of v5, /device:TPU:0, one launch (start us, length us, event | category | flops | bytes accessed | tf_op | source)
XLA Modules:
  0.0 202.9 jit_solution(18121438525770965122)
XLA Ops:
  0.7 195.2 %step.1 = (bf16[512,512]{1,0:T(8,128)(2,1)}, f32[512,512]{1,0:T(8,128)}, bf16[5,2,1824,128]{3,2,1,0:T(8,128)(2,1)}, bf16[2224,128]{1,0:T(8,128)(2,1)}, f32[112,128]{1,0:T(8,128)}) custom-call(bf16[512,512]{1,0:T(8,128)(2,1)} %refs_0_.1, bf16[64,512]{1,0:T(8,128)(2,1)} %bitcast.38, s32[1,512]{1,0:T(1,128)} %bitcast.46, s32[1,512]{1,0:T(1,128)} %bitcast.47, ...), custom_call_target="tpu_custom_call" | custom-call | tf_op jit(solution)/shard_map/step/pallas_call | solution.py:961
  195.8 6.9 %finish.1 = (bf16[512,512]{1,0:T(8,128)(2,1)}, f32[512,512]{1,0:T(8,128)}, f32[6,672,128]{2,1,0:T(8,128)}, f32[6,1024,128]{2,1,0:T(8,128)}, f32[128,512]{1,0:T(8...) custom-call(bf16[5,2,1824,128]{3,2,1,0:T(8,128)(2,1)} %get-tuple-ele, ...), custom_call_target="tpu_custom_call" | custom-call | tf_op jit(solution)/shard_map/finish/pallas_call | solution.py:1038

commit v6 on v5

--- a/solution.py
+++ b/solution.py
@@ -143,7 +143,7 @@
     before = jnp.maximum(section - 1, 0)
     chunks = rows // CHUNK
     jobs = jnp.where(edge, 2, 3)
-    held = (section == steps - 1) & edge
+    held = (section >= steps - 2) & edge
     farthest = CHIPS - 1 - chip
     first_head = jnp.where(edge, 1, 3)
 
@@ -744,19 +744,19 @@
         def _():
             weight_grads(jnp.minimum(turn, jobs - 1), True)
 
+            @pl.when((turn >= jobs - 1) & (chip > 0))
+            def _():
+                pl.semaphore_signal(up_ok, inc=1, device_id=at_chip(jnp.maximum(chip - 1, 0)), device_id_type=MESH)
+
+            @pl.when((turn >= jobs - 1) & (chip < CHIPS - 1))
+            def _():
+                pl.semaphore_signal(
+                    dn_ok, inc=1, device_id=at_chip(jnp.minimum(chip + 1, CHIPS - 1)), device_id_type=MESH
+                )
+
         return carry
 
     lax.fori_loop(0, jobs + 1, turns, 0)
-
-    @pl.when(chip > 0)
-    def _():
-        pl.semaphore_signal(up_ok, inc=1, device_id=at_chip(jnp.maximum(chip - 1, 0)), device_id_type=MESH)
-
-    @pl.when(chip < CHIPS - 1)
-    def _():
-        pl.semaphore_signal(
-            dn_ok, inc=1, device_id=at_chip(jnp.minimum(chip + 1, CHIPS - 1)), device_id_type=MESH
-        )
 
     @pl.when(chip < CHIPS - 1)
     def _():

time: 203 us -> 202 us (level)
  the two profiles are of different devices: /device:TPU:0 before, /device:TPU:14 now
where the time goes in v6:
time: 202 us; the launch traced here: 199 us
  Pallas kernels  198 us (98%)
    pallas_call x1, Pallas kernels, on_device(): pl.pallas_call(functools.partial(step_kernel, dims), out_shape=[jax.Shape...  191 us
    pallas_call x1, Pallas kernels, on_device(): pl.pallas_call(functools.partial(finish_kernel, (lat, in_width, hid, head...  6.91 us

profile of v6, /device:TPU:14, one launch (start us, length us, event | category | flops | bytes accessed | tf_op | source)
XLA Modules:
  0.0 198.8 jit_solution(2946857250225887938)
XLA Ops:
  0.7 191.1 %step.1 = (bf16[512,512]{1,0:T(8,128)(2,1)}, f32[512,512]{1,0:T(8,128)}, bf16[5,2,1824,128]{3,2,1,0:T(8,128)(2,1)}, bf16[2224,128]{1,0:T(8,128)(2,1)}, f32[112,128]{1,0:T(8,128)}) custom-call(bf16[512,512]{1,0:T(8,128)(2,1)} %refs_0_.1, bf16[64,512]{1,0:T(8,128)(2,1)} %bitcast.38, s32[1,512]{1,0:T(1,128)} %bitcast.46, s32[1,512]{1,0:T(1,128)} %bitcast.47, ...), custom_call_target="tpu_custom_call" | custom-call | tf_op jit(solution)/shard_map/step/pallas_call | solution.py:961
  191.7 6.9 %finish.1 = (bf16[512,512]{1,0:T(8,128)(2,1)}, f32[512,512]{1,0:T(8,128)}, f32[6,672,128]{2,1,0:T(8,128)}, f32[6,1024,128]{2,1,0:T(8,128)}, f32[128,512]{1,0:T(8...) custom-call(bf16[5,2,1824,128]{3,2,1,0:T(8,128)(2,1)} %get-tuple-ele, ...), custom_call_target="tpu_custom_call" | custom-call | tf_op jit(solution)/shard_map/finish/pallas_call | solution.py:1038

commit v7 on v6

--- a/solution.py
+++ b/solution.py
@@ -492,7 +492,9 @@
         def order(i):
             far_first = jnp.where(lower, CHIPS - 1 - i, i)
             pair_first = lax.rem(jnp.where(lower, CHIPS - i, i + CHIPS - 1), CHIPS)
-            return jnp.where(edge, far_first, pair_first)
+            if not q:
+                return far_first
+            return jnp.where(edge | ((section == last) & (job == jobs - 1)), far_first, pair_first)
 
         def make(z):
             cols = pl.ds(pl.multiple_of(z * 2 * LANES, 2 * LANES), 2 * LANES)

time: 202 us -> 202 us (level)
  no operation moved by 1% of the time
where the time goes in v7:
time: 202 us; the launch traced here: 199 us
  Pallas kernels  198 us (98%)
    pallas_call x1, Pallas kernels, on_device(): pl.pallas_call(functools.partial(step_kernel, dims), out_shape=[jax.Shape...  191 us
    pallas_call x1, Pallas kernels, on_device(): pl.pallas_call(functools.partial(finish_kernel, (lat, in_width, hid, head...  6.91 us

profile of v7, /device:TPU:14, one launch (start us, length us, event | category | flops | bytes accessed | tf_op | source)
XLA Modules:
  0.0 198.8 jit_solution(6087687734545314283)
XLA Ops:
  0.7 191.1 %step.1 = (bf16[512,512]{1,0:T(8,128)(2,1)}, f32[512,512]{1,0:T(8,128)}, bf16[5,2,1824,128]{3,2,1,0:T(8,128)(2,1)}, bf16[2224,128]{1,0:T(8,128)(2,1)}, f32[112,128]{1,0:T(8,128)}) custom-call(bf16[512,512]{1,0:T(8,128)(2,1)} %refs_0_.1, bf16[64,512]{1,0:T(8,128)(2,1)} %bitcast.38, s32[1,512]{1,0:T(1,128)} %bitcast.46, s32[1,512]{1,0:T(1,128)} %bitcast.47, ...), custom_call_target="tpu_custom_call" | custom-call | tf_op jit(solution)/shard_map/step/pallas_call | solution.py:963
  191.7 6.9 %finish.1 = (bf16[512,512]{1,0:T(8,128)(2,1)}, f32[512,512]{1,0:T(8,128)}, f32[6,672,128]{2,1,0:T(8,128)}, f32[6,1024,128]{2,1,0:T(8,128)}, f32[128,512]{1,0:T(8...) custom-call(bf16[5,2,1824,128]{3,2,1,0:T(8,128)(2,1)} %get-tuple-ele, ...), custom_call_target="tpu_custom_call" | custom-call | tf_op jit(solution)/shard_map/finish/pallas_call | solution.py:1040
